TPU v7x, 256 devices: a whole 4x4x8 slice. The times are simulated.
256 devices in a mesh: dp: 32 (over y, z), tensor: 8 (over x, core).
Axes of the slice: x: 4, y: 4, z: 8, core: 2. Of those that a mesh axis runs over, the one named last changes fastest.
Arguments:
- new_states: bfloat16 [8192, 4, 5120], P(('dp', 'tensor')), may hold values from -6 to 6
- w_query: bfloat16 [5120, 4096], P(None, 'tensor'), may hold values from -0.078125 to 0.078125
- keyvalue_weight: bfloat16 [5120, 16, 128], P(None, 'tensor'), may hold values from -0.078125 to 0.078125
- keyvalue_pages: bfloat16 [1024, 16, 128, 128], P('dp', 'tensor'), may hold values from -110 to 110
- page_table: int32 [32, 32], P('dp'), may hold values from 0 to 31, each once within a row
- prompt_pages: int32 [32, 8], P('dp'), may hold values from 1 to 4, as said below
- share_prompt: int32 [32, 32], P('dp'), may hold values from 0 to 7, never falling along the last dimension, each value on 1 to 8 neighbouring positions
- share_group: int32 [32, 32], P('dp'), may hold values from 0 to 31, each once within a row
Outputs:
- attended: bfloat16 [8192, 4, 4096], P('dp', None, 'tensor')
Inputs may be any that keep to these rules, and one draw needn't show every extreme that they name: `share_prompt`: each owner's shares of one prompt are consecutive, from 1 to 8 shares a prompt, so that a prompt has 8 to 64 samples; every prompt has a share. `share_group`: each row names every group once: every group decodes exactly one share of every owner. `page_table`: each row is a permutation of the owner's pages. `prompt_pages`: some prompt has exactly 4 pages and some exactly one.
All inputs are finite; a program needn't handle non-finite values.
Results may differ from a plain program's by a relative error of at most 0.012.
The roundings to bfloat16 on the way count: a program that leaves them out, or rounds other values in their place, can miss the bound.
Values may be sent and summed in bfloat16 or wider, within the bound.
No kernel may reach another device: no remote copies, remote signals or barrier semaphores. Data moves between devices by JAX's collectives and lax.ppermute only.
A program may use at most 192 MiB of HBM per device.

v0:
```python
import functools
import math

import jax
import jax.numpy as jnp
from jax import lax
from jax.experimental import pallas as pl
from jax.experimental.pallas import tpu as pltpu
from jax.sharding import PartitionSpec as P

HEAD_SIZE = 128
PAGE_TOKENS = 128
LONGEST_PAGES = 4
PROMPT_SAMPLES = 8
STEPS = 4
EPSILON = 1e-06

Y, Z, X, C = 4, 8, 4, 2
SLAB = PROMPT_SAMPLES * STEPS
OWNERS = 32
HEADS = 4
TILE = HEADS * SLAB
STAT_ROWS = 16
MiB = 1024 * 1024


def along_x(step):
    return [(x * C + c, (x + step) % X * C + c) for x in range(X) for c in range(C)]


def other_core():
    return [(i, i ^ 1) for i in range(X * C)]


def rope_tables():
    half = HEAD_SIZE // 2
    freqs = jnp.exp(
        -(2.0 * jnp.arange(half, dtype=jnp.float32) / HEAD_SIZE) * jnp.log(1000000.0)
    )
    pages = jnp.arange(1, LONGEST_PAGES + 1, dtype=jnp.int32)[:, None]
    steps = jnp.arange(2 * STEPS, dtype=jnp.int32)[None, :] % STEPS
    angles = (PAGE_TOKENS * pages + steps).astype(jnp.float32)[..., None] * freqs
    cosine, sine = jnp.cos(angles), jnp.sin(angles)
    return (
        jnp.concatenate([cosine, cosine], axis=-1),
        jnp.concatenate([-sine, sine], axis=-1),
    )


def rotated(values, cosine, sine):
    values = values * lax.rsqrt(jnp.mean(values * values, axis=-1, keepdims=True) + EPSILON)
    turned = pltpu.roll(values, HEAD_SIZE // 2, 1)
    fold = (SLAB // 8, 8, HEAD_SIZE)
    out = values.reshape(fold) * cosine[None] + turned.reshape(fold) * sine[None]
    return out.reshape(SLAB, HEAD_SIZE)


def norm_kernel(states, slab, held, scratch, sem):
    load = pltpu.make_async_copy(states, held, sem)
    load.start()
    load.wait()
    for r in range(states.shape[0]):
        flat = held[r].astype(jnp.float32)
        flat = flat * lax.rsqrt(jnp.mean(flat * flat, axis=-1, keepdims=True) + EPSILON)
        scratch[r * STEPS:(r + 1) * STEPS, :] = flat
    slab[...] = scratch[...].astype(jnp.bfloat16)


def forward_kernel(ahead, behind, *refs):
    both, far_0, far_1 = refs[-3:]
    half = ahead.shape[0] // 2
    both[:2 * half] = behind[...]
    both[2 * half:] = ahead[...]
    far_0[...] = ahead[:half]
    far_1[...] = behind[half:]


def join_kernel(far_0, far_1, after, far):
    half = far_0.shape[0]
    far[:half] = far_0[...]
    far[half:] = far_1[...]


def project(place, counts, deltas, mine, theirs, wq, wkv, cos_ref, sin_ref, put):
    x, c = place[0], place[1]
    states = jnp.concatenate([mine, theirs], axis=0)
    slots = []
    for side in range(2):
        for number, delta in enumerate(deltas):
            for j in range(4):
                within = 4 * (c ^ side) + j
                n = counts[Z * ((x + delta) % X) + within]
                slots.append((number, within, cos_ref[n - 1], sin_ref[n - 1]))
    for block in range(3):
        weight = wq[:, block * 256:block * 256 + 256] if block < 2 else wkv[...]
        raw = jnp.dot(states, weight, preferred_element_type=jnp.float32)
        for slot, (number, within, cosine, sine) in enumerate(slots):
            rows = raw[slot * SLAB:(slot + 1) * SLAB]
            first, second = rows[:, :HEAD_SIZE], rows[:, HEAD_SIZE:]
            first = rotated(first, cosine, sine).astype(jnp.bfloat16)
            if block < 2:
                second = rotated(second, cosine, sine)
            second = second.astype(jnp.bfloat16)
            put(number, within, 2 * block, first)
            put(number, within, 2 * block + 1, second)


def near_kernel(deltas, place, counts, *refs):
    slabs, (wq, wkv, cos_ref, sin_ref, near) = refs[:-5], refs[-5:]

    def put(number, within, kind, rows):
        near[number, within, pl.ds(kind * SLAB, SLAB), :] = rows

    mine, theirs = [slab[...] for slab in slabs]
    project(place, counts, deltas, mine, theirs, wq, wkv, cos_ref, sin_ref, put)


def far_kernel(place, counts, *refs):
    slabs, (wq, wkv, cos_ref, sin_ref, first, near, queries, keyvals) = refs[:2], refs[2:]
    x = place[0]

    def put(number, within, kind, rows):
        owner = Z * ((x + 2) % X) + within
        if kind < HEADS:
            queries[owner, pl.ds(kind * SLAB, SLAB), :] = rows
        else:
            keyvals[owner, pl.ds((kind - HEADS) * SLAB, SLAB), :] = rows

    mine, theirs = [slab[...] for slab in slabs]
    project(place, counts, (2,), mine, theirs, wq, wkv, cos_ref, sin_ref, put)
    for piece, delta in ((first.at[0], 0), (near.at[0], 1), (near.at[1], 3)):
        for within in range(Z):
            owner = Z * ((x + delta) % X) + within
            queries[owner] = piece[within, :TILE]
            keyvals[owner] = piece[within, TILE:]


def newest_kernel(queries, keyvals, numer_ref, stat_ref):
    token = lax.broadcasted_iota(jnp.int32, (SLAB, TILE), 0)
    line = lax.broadcasted_iota(jnp.int32, (SLAB, TILE), 1) % SLAB
    seen = (line // STEPS == token // STEPS) & (token <= line)

    def some(step, carry):
        owners = [step * 8 + i for i in range(8)]
        scores = [
            lax.dot_general(
                keyvals[owner, :SLAB], queries[owner], (((1,), (1,)), ((), ())),
                preferred_element_type=jnp.float32,
            )
            for owner in owners
        ]
        mass = []
        for owner, score in zip(owners, scores):
            score = jnp.where(seen, score * (1.0 / math.sqrt(HEAD_SIZE)), -jnp.inf)
            peak = jnp.max(score, axis=0, keepdims=True)
            mass.append(jnp.exp(score - peak))
            stat_ref[owner, 0:1, :] = peak
            stat_ref[owner, 1:2, :] = jnp.sum(mass[-1], axis=0, keepdims=True)
        for owner, weights in zip(owners, mass):
            numer_ref[owner] = jnp.dot(
                weights.T.astype(jnp.bfloat16), keyvals[owner, SLAB:],
                preferred_element_type=jnp.float32,
            ).astype(jnp.bfloat16)
        return carry

    lax.fori_loop(0, OWNERS // 8, some, 0)


def prompt_kernel(tables, counts, queries, pages, answers):
    eye = diagonal()
    row = lax.broadcasted_iota(jnp.int32, (STAT_ROWS, HEAD_SIZE), 0)
    token = lax.broadcasted_iota(jnp.int32, (TILE, LONGEST_PAGES * PAGE_TOKENS), 1)
    scale = math.log2(math.e) / math.sqrt(HEAD_SIZE)

    def some(step, carry):
        groups = [step * 4 + i for i in range(4)]
        at = [[tables[g * LONGEST_PAGES + page] for page in range(LONGEST_PAGES)] for g in groups]
        scores = []
        for i, g in enumerate(groups):
            keys = jnp.concatenate([pages[p, 0] for p in at[i]], axis=0)
            scores.append(
                lax.dot_general(
                    queries[g], keys, (((1,), (1,)), ((), ())), preferred_element_type=jnp.float32
                )
            )
        mass, total, logs = [], [], []
        for g, score in zip(groups, scores):
            score = jnp.where(token < counts[g] * PAGE_TOKENS, score, -jnp.inf)
            peak = jnp.max(score, axis=-1, keepdims=True)
            mass.append(jnp.exp2((score - peak) * scale))
            total.append(jnp.sum(mass[-1], axis=-1, keepdims=True))
            logs.append(peak * (1.0 / math.sqrt(HEAD_SIZE)) + jnp.log(total[-1]))
        for i, g in enumerate(groups):
            values = jnp.concatenate([pages[p, 1] for p in at[i]], axis=0)
            numer = jnp.dot(mass[i].astype(jnp.bfloat16), values, preferred_element_type=jnp.float32)
            answers[g, pl.ds(0, TILE), :] = (numer / total[i]).astype(jnp.bfloat16)
            flat = jnp.sum(jnp.where(eye, logs[i], 0.0), axis=0, keepdims=True)
            stats = jnp.zeros((STAT_ROWS, HEAD_SIZE), jnp.float32)
            for piece in range(3):
                rounded = flat.astype(jnp.bfloat16).astype(jnp.float32)
                stats = jnp.where(row == piece, rounded, stats)
                flat = flat - rounded
            answers[g, pl.ds(TILE, STAT_ROWS), :] = stats.astype(jnp.bfloat16)
        return carry

    lax.fori_loop(0, OWNERS // 4, some, 0)


def merge_kernel(back, numer_ref, stat_ref, out):
    eye = diagonal()

    def some(step, carry):
        for i in range(4):
            owner = step * 4 + i
            stats = back[owner, pl.ds(TILE, STAT_ROWS), :].astype(jnp.float32)
            log_p = stats[0:1] + (stats[1:2] + stats[2:3])
            peak_n, total_n = stat_ref[owner, 0:1, :], stat_ref[owner, 1:2, :]
            log_n = peak_n + jnp.log(total_n)
            top = jnp.maximum(log_p, log_n)
            first, second = jnp.exp(log_p - top), jnp.exp(log_n - top)
            share_p = first / (first + second)
            share_n = second / ((first + second) * total_n)
            share_p = jnp.sum(jnp.where(eye, share_p, 0.0), axis=1, keepdims=True)
            share_n = jnp.sum(jnp.where(eye, share_n, 0.0), axis=1, keepdims=True)
            prompt = back[owner, pl.ds(0, TILE), :].astype(jnp.float32)
            newest = numer_ref[owner].astype(jnp.float32)
            merged = (prompt * share_p + newest * share_n).astype(jnp.bfloat16)
            for j in range(HEADS):
                out[owner, :, pl.ds(j * HEAD_SIZE, HEAD_SIZE)] = merged[j * SLAB:(j + 1) * SLAB]
        return carry

    lax.fori_loop(0, OWNERS // 4, some, 0)


def diagonal():
    first = lax.broadcasted_iota(jnp.int32, (TILE, HEAD_SIZE), 0)
    return first == lax.broadcasted_iota(jnp.int32, (TILE, HEAD_SIZE), 1)


VMEM = pl.BlockSpec(memory_space=pltpu.VMEM)
SMEM = pl.BlockSpec(memory_space=pltpu.SMEM)
ANY = pl.BlockSpec(memory_space=pl.ANY)


def params(mib):
    return pltpu.CompilerParams(vmem_limit_bytes=mib * MiB)


def body(
    new_states,
    w_query,
    keyvalue_weight,
    keyvalue_pages,
    page_table,
    prompt_pages,
    share_prompt,
    share_group,
):
    groups = lax.axis_size("dp")
    width = new_states.shape[2]
    tensor = lax.axis_index("tensor")
    place = jnp.stack([tensor // C, tensor % C]).astype(jnp.int32)

    targets = jnp.arange(groups, dtype=jnp.int32)
    match = (share_group[0][:, None] == targets[None, :]).astype(jnp.int32)
    dest_prompt = jnp.sum(match * share_prompt[0][:, None], axis=0)
    choose = (
        dest_prompt[:, None] == jnp.arange(prompt_pages.shape[1], dtype=jnp.int32)[None, :]
    ).astype(jnp.int32)
    dest_count = jnp.sum(choose * prompt_pages[0][None, :], axis=1)
    logical = (
        dest_prompt[:, None] * LONGEST_PAGES + jnp.arange(LONGEST_PAGES, dtype=jnp.int32)[None, :]
    )
    lookup = (
        logical[:, :, None] == jnp.arange(page_table.shape[1], dtype=jnp.int32)[None, None, :]
    ).astype(jnp.int32)
    physical = jnp.sum(lookup * page_table[0][None, None, :], axis=2).reshape(-1)
    slot_count = lax.all_to_all(dest_count, "dp", split_axis=0, concat_axis=0, tiled=True)
    cosine, sine = rope_tables()
    wkv = keyvalue_weight.reshape(width, -1)

    rows = new_states.shape[0] * STEPS
    own = pl.pallas_call(
        norm_kernel,
        out_shape=jax.ShapeDtypeStruct((rows, width), jnp.bfloat16),
        in_specs=[ANY],
        out_specs=VMEM,
        scratch_shapes=[
            pltpu.VMEM(new_states.shape, jnp.bfloat16),
            pltpu.VMEM((rows, width), jnp.float32),
            pltpu.SemaphoreType.DMA,
        ],
        compiler_params=params(8),
        name="norm",
    )(new_states)
    ahead = lax.ppermute(own, "tensor", along_x(1))
    behind = lax.ppermute(own, "tensor", along_x(-1))
    own_theirs = lax.ppermute(own, "tensor", other_core())

    def project_near(deltas, *slabs):
        return pl.pallas_call(
            functools.partial(near_kernel, deltas),
            out_shape=jax.ShapeDtypeStruct(
                (len(deltas), Z, TILE + 2 * SLAB, HEAD_SIZE), jnp.bfloat16
            ),
            in_specs=[SMEM] * 2 + [VMEM] * (len(slabs) + 4),
            out_specs=VMEM,
            compiler_params=params(16),
            name="project_near",
        )(place, slot_count, *slabs, w_query, wkv, cosine, sine)

    first = project_near((0,), own, own_theirs)
    half = jax.ShapeDtypeStruct((rows // 2, width), jnp.bfloat16)
    both, far_0, far_1 = pl.pallas_call(
        forward_kernel,
        out_shape=(jax.ShapeDtypeStruct((2 * rows, width), jnp.bfloat16), half, half),
        in_specs=[VMEM] * 3,
        out_specs=(VMEM,) * 3,
        compiler_params=params(4),
        name="forward",
    )(ahead, behind, first)
    far_0 = lax.ppermute(far_0, "tensor", along_x(1))
    far_1 = lax.ppermute(far_1, "tensor", along_x(-1))
    both_theirs = lax.ppermute(both, "tensor", other_core())
    near = project_near((1, 3), both, both_theirs)

    far = pl.pallas_call(
        join_kernel,
        out_shape=jax.ShapeDtypeStruct((rows, width), jnp.bfloat16),
        in_specs=[VMEM] * 3,
        out_specs=VMEM,
        compiler_params=params(4),
        name="join",
    )(far_0, far_1, near)
    far_theirs = lax.ppermute(far, "tensor", other_core())
    queries, keyvals = pl.pallas_call(
        far_kernel,
        out_shape=(
            jax.ShapeDtypeStruct((OWNERS, TILE, HEAD_SIZE), jnp.bfloat16),
            jax.ShapeDtypeStruct((OWNERS, 2 * SLAB, HEAD_SIZE), jnp.bfloat16),
        ),
        in_specs=[SMEM] * 2 + [VMEM] * 8,
        out_specs=(VMEM,) * 2,
        compiler_params=params(12),
        name="project_far",
    )(place, slot_count, far, far_theirs, w_query, wkv, cosine, sine, first, near)

    asked = lax.all_to_all(queries, "dp", split_axis=0, concat_axis=0, tiled=True)
    newest = pl.pallas_call(
        newest_kernel,
        out_shape=(
            jax.ShapeDtypeStruct((OWNERS, TILE, HEAD_SIZE), jnp.bfloat16),
            jax.ShapeDtypeStruct((OWNERS, 8, TILE), jnp.float32),
        ),
        in_specs=[VMEM] * 2,
        out_specs=(VMEM,) * 2,
        compiler_params=params(8),
        name="newest_tokens",
    )(queries, keyvals)
    answers = pl.pallas_call(
        prompt_kernel,
        out_shape=jax.ShapeDtypeStruct((OWNERS, TILE + STAT_ROWS, HEAD_SIZE), jnp.bfloat16),
        in_specs=[SMEM] * 2 + [VMEM] * 2,
        out_specs=VMEM,
        compiler_params=params(8),
        name="prompt_attention",
    )(physical, dest_count, asked, keyvalue_pages)
    back = lax.all_to_all(answers, "dp", split_axis=0, concat_axis=0, tiled=True)
    out = pl.pallas_call(
        merge_kernel,
        out_shape=jax.ShapeDtypeStruct((OWNERS, SLAB, HEADS * HEAD_SIZE), jnp.bfloat16),
        in_specs=[VMEM] * 3,
        out_specs=VMEM,
        compiler_params=params(8),
        name="merge",
    )(back, *newest)
    return out.reshape(groups * PROMPT_SAMPLES, STEPS, HEADS * HEAD_SIZE)


def solution(mesh):
    placed = (
        P(("dp", "tensor"), None, None),
        P(None, "tensor"),
        P(None, "tensor", None),
        P("dp", "tensor", None, None),
        P("dp", None),
        P("dp", None),
        P("dp", None),
        P("dp", None),
    )
    return jax.shard_map(
        body, mesh=mesh, in_specs=placed, out_specs=P("dp", None, "tensor"), check_vma=False
    )
```

profile of v0, /device:TPU:6, one launch (start us, length us, event | category | flops | bytes accessed | tf_op | source)
XLA Modules:
  0.0 152.3 jit_solution(4165506287340643029)
XLA Ops:
  0.0 1.3 copy-done.4
  1.3 1.1 norm.1.refs_0_
  2.5 0.1 collective-permute-start.2
  2.6 0.9 collective-permute-start.1
  3.5 2.4 %collective-permute-start = (bf16[128,5120]{1,0:T(8,128)(2,1)S(1)}, bf16[128,5120]{1,0:T(8,128)(2,1)}, u32[]{:S(2)}, u32[]{:S(2)}) collective-permute-start(bf16[128,5120]{1,0:T(8,128)(2,1)S(1)} %norm.1.refs_0_), channel_id=1, source_target_pairs={{0,2},{1,3},{2,4},{3,5},{4,6},{5,7},{6,0},{7,1},{8,10},{9,11},{10,... | collective-permute-start | bytes 3932168 | tf_op jit(solution)/shard_map/ppermute | solution.py:296
  5.9 0.1 select_reduce_fusion.1
  6.0 0.1 select_reduce_fusion.2.counts
  6.1 0.7 copy.12
  6.8 11.5 %all-to-all-start = ((s32[32,1,1]{2,1,0:T(1,128)}), s32[32,1,1]{2,1,0:T(1,128)S(1)}, u32[]{:S(2)}, u32[]{:S(2)}) async-start(s32[32,1,1]{2,1,0:T(1,128)} %copy.12), calls=%async_computation | async-start | bytes 32768 | tf_op jit(solution)/shard_map/all_to_all | solution.py:278
  18.3 0.1 add_convert_fusion
  18.4 0.1 fusion
  18.5 0.1 pad_maximum_fusion
  18.6 0.1 pad_add_fusion.place
  18.7 3.7 %copy.15 = bf16[640,8,2,128]{3,1,2,0:T(8,128)(2,1)} copy(bf16[640,8,2,128]{3,2,1,0:T(2,128)(2,1)} %bitcast.17) | data formatting | bytes 5242880
  22.4 5.6 %all-to-all-done = s32[32,1,1]{2,1,0:T(1,128)S(1)} async-done(((s32[32,1,1]{2,1,0:T(1,128)}), s32[32,1,1]{2,1,0:T(1,128)S(1)}, u32[]{:S(2)}, u32[]{:S(2)}) %all-to-all-start) | async-done | bytes 160 | tf_op jit(solution)/shard_map/all_to_all | solution.py:278
  28.0 0.7 reduce.counts
  28.6 0.0 collective-permute-done.2.refs_1_
  28.7 0.0 copy-start
  28.7 2.5 %copy-done = bf16[5120,512]{1,0:T(8,128)(2,1)S(1)} copy-done((bf16[5120,512]{1,0:T(8,128)(2,1)S(1)}, bf16[5120,512]{1,0:T(8,128)(2,1)}, u32[]{:S(2)}) %copy-start) | copy-done | bytes 5242904
  31.1 1.7 %copy-done.1 = bf16[640,8,2,128]{3,1,2,0:T(8,128)(2,1)S(1)} copy-done((bf16[640,8,2,128]{3,1,2,0:T(8,128)(2,1)S(1)}, bf16[640,8,2,128]{3,1,2,0:T(8,128)(2,1)}, u32[]{:S(2)}) %copy-start.1) | copy-done | bytes 2621464
  32.9 4.0 %project_near.2.refs_0_.refs_6_ = bf16[1,8,192,128]{3,2,1,0:T(8,128)(2,1)S(1)} custom-call(s32[2]{0:T(128)S(1)} %pad_add_fusion.place, s32[32]{0:T(128)S(1)} %reduce.counts, bf16[128,5120]{1,0:T(8,128)(2,1)S(1)} %norm.1.refs_0_, bf16[128,5120]{1,0:T(8,128)(2,1)} %collective-permute-done.2.refs_1_, bf16[5120,512]{1,0:T(8,128)(2,1)S(1)} %copy-done, ...), custom_call_target="tpu_custom_call" | custom-call | tf_op jit(solution)/shard_map/project_near/pallas_call | solution.py:301
  36.9 0.0 collective-permute-done.1.behind
  36.9 0.0 collective-permute-done.ahead
  36.9 2.1 %forward.1 = (bf16[256,5120]{1,0:T(8,128)(2,1)S(1)}, bf16[64,5120]{1,0:T(8,128)(2,1)S(1)}, bf16[64,5120]{1,0:T(8,128)(2,1)S(1)}) custom-call(bf16[128,5120]{1,0:T(8,128)(2,1)} %collective-permute-done.ahead, bf16[128,5120]{1,0:T(8,128)(2,1)} %collective-permute-done.1.behind, bf16[1,8,192,128]{3,2,1,0:T(8,128)(2,1)S(1)} %project_near.2.refs_0_.refs_6_), custom_call_target="tpu_custom_call" | custom-call | tf_op jit(solution)/shard_map/forward/pallas_call | solution.py:314
  39.0 0.1 collective-permute-start.5
  39.1 1.1 collective-permute-start.3
  40.2 1.0 collective-permute-start.4
  41.2 2.8 %collective-permute-done.5.refs_1_ = bf16[256,5120]{1,0:T(8,128)(2,1)S(1)} collective-permute-done((bf16[256,5120]{1,0:T(8,128)(2,1)S(1)}, bf16[256,5120]{1,0:T(8,128)(2,1)S(1)}, u32[]{:S(2)}, u32[]{:S(2)}) %collective-permute-start.5) | collective-permute-done | bytes 2621472 | tf_op jit(solution)/shard_map/ppermute | solution.py:324
  44.0 0.0 slice-done.1
  44.0 5.4 %project_near.3.after.refs_7_ = bf16[2,8,192,128]{3,2,1,0:T(8,128)(2,1)S(1)} custom-call(s32[2]{0:T(128)S(1)} %pad_add_fusion.place, s32[32]{0:T(128)S(1)} %reduce.counts, bf16[256,5120]{1,0:T(8,128)(2,1)S(1)} %get-tuple-element.14.refs_0_, bf16[256,5120]{1,0:T(8,128)(2,1)S(1)} %collective-permute-done.5.refs_1_, bf16[5120,512]{1,0:T(8,128)(2,1)S(1)} %bitcast.12, ...), custom_call_target="tpu_custom_call" | custom-call | tf_op jit(solution)/shard_map/project_near/pallas_call | solution.py:301
  49.5 6.8 %collective-permute-done.3.far_0 = bf16[64,5120]{1,0:T(8,128)(2,1)S(1)} collective-permute-done((bf16[64,5120]{1,0:T(8,128)(2,1)S(1)}, bf16[64,5120]{1,0:T(8,128)(2,1)S(1)}, u32[]{:S(2)}, u32[]{:S(2)}) %collective-permute-start.3) | collective-permute-done | bytes 655392 | tf_op jit(solution)/shard_map/ppermute | solution.py:322
  56.3 1.9 %collective-permute-done.4.far_1 = bf16[64,5120]{1,0:T(8,128)(2,1)S(1)} collective-permute-done((bf16[64,5120]{1,0:T(8,128)(2,1)S(1)}, bf16[64,5120]{1,0:T(8,128)(2,1)S(1)}, u32[]{:S(2)}, u32[]{:S(2)}) %collective-permute-start.4) | collective-permute-done | bytes 655392 | tf_op jit(solution)/shard_map/ppermute | solution.py:323
  58.2 0.1 join.1.refs_0_
  58.3 0.1 collective-permute-start.6
  58.4 3.0 %collective-permute-done.6.refs_1_ = bf16[128,5120]{1,0:T(8,128)(2,1)S(1)} collective-permute-done((bf16[128,5120]{1,0:T(8,128)(2,1)S(1)}, bf16[128,5120]{1,0:T(8,128)(2,1)S(1)}, u32[]{:S(2)}, u32[]{:S(2)}) %collective-permute-start.6) | collective-permute-done | bytes 1310752 | tf_op jit(solution)/shard_map/ppermute | solution.py:335
  61.4 4.1 %project_far.1 = (bf16[32,128,128]{2,1,0:T(8,128)(2,1)}, bf16[32,64,128]{2,1,0:T(8,128)(2,1)S(1)}) custom-call(s32[2]{0:T(128)S(1)} %pad_add_fusion.place, s32[32]{0:T(128)S(1)} %reduce.counts, bf16[128,5120]{1,0:T(8,128)(2,1)S(1)} %join.1.refs_0_, bf16[128,5120]{1,0:T(8,128)(2,1)S(1)} %collective-permute-done.6.refs_1_, bf16[5120,512]{1,0:T(8,128)(2,1)S(1)} %bitcast.12, ...), custom_call_target="tpu_custom_call" | custom-call | tf_op jit(solution)/shard_map/project_far/pallas_call | solution.py:336
  65.5 0.8 copy-done.5
  66.3 11.6 %all-to-all-start.1 = ((bf16[32,128,128]{2,1,0:T(8,128)(2,1)}), bf16[32,128,128]{2,1,0:T(8,128)(2,1)S(1)}, u32[]{:S(2)}, u32[]{:S(2)}) async-start(bf16[32,128,128]{2,1,0:T(8,128)(2,1)} %get-tuple-element.15.queries), calls=%async_computation.1 | async-start | bytes 2097152 | tf_op jit(solution)/shard_map/all_to_all | solution.py:348
  77.9 0.2 select_reduce_fusion
  78.2 0.1 copy.11
  78.3 0.1 reshape.95.tables
  78.4 28.4 %all-to-all-done.1.queries = bf16[32,128,128]{2,1,0:T(8,128)(2,1)S(1)} async-done(((bf16[32,128,128]{2,1,0:T(8,128)(2,1)}), bf16[32,128,128]{2,1,0:T(8,128)(2,1)S(1)}, u32[]{:S(2)}, u32[]{:S(2)}) %all-to-all-start.1) | async-done | bytes 1048608 | tf_op jit(solution)/shard_map/all_to_all | solution.py:348
  106.8 6.2 %prompt_attention.1 = bf16[32,144,128]{2,1,0:T(8,128)(2,1)} custom-call(s32[128]{0:T(128)S(1)} %reshape.95.tables, s32[32]{0:T(128)S(1)} %select_reduce_fusion.2.counts, bf16[32,128,128]{2,1,0:T(8,128)(2,1)S(1)} %all-to-all-done.1.queries, bf16[32,2,128,128]{3,2,1,0:T(8,128)(2,1)S(1)} %copy-done.3), custom_call_target="tpu_custom_call" | custom-call | tf_op jit(solution)/shard_map/prompt_attention/pallas_call | solution.py:360
  113.1 5.2 %all-to-all-start.2 = ((bf16[32,144,128]{2,1,0:T(8,128)(2,1)}), bf16[32,144,128]{2,1,0:T(8,128)(2,1)S(1)}, u32[]{:S(2)}, u32[]{:S(2)}) async-start(bf16[32,144,128]{2,1,0:T(8,128)(2,1)} %prompt_attention.1), calls=%async_computation.2 | async-start | bytes 2359296 | tf_op jit(solution)/shard_map/all_to_all | solution.py:368
  118.3 3.2 %newest_tokens.1 = (bf16[32,128,128]{2,1,0:T(8,128)(2,1)S(1)}, f32[32,8,128]{2,1,0:T(8,128)S(1)}) custom-call(bf16[32,128,128]{2,1,0:T(8,128)(2,1)} %get-tuple-element.15.queries, bf16[32,64,128]{2,1,0:T(8,128)(2,1)S(1)} %copy-done.6), custom_call_target="tpu_custom_call" | custom-call | tf_op jit(solution)/shard_map/newest_tokens/pallas_call | solution.py:349
  121.5 27.8 %all-to-all-done.2.back = bf16[32,144,128]{2,1,0:T(8,128)(2,1)S(1)} async-done(((bf16[32,144,128]{2,1,0:T(8,128)(2,1)}), bf16[32,144,128]{2,1,0:T(8,128)(2,1)S(1)}, u32[]{:S(2)}, u32[]{:S(2)}) %all-to-all-start.2) | async-done | bytes 1179680 | tf_op jit(solution)/shard_map/all_to_all | solution.py:368
  149.3 1.9 %merge.1 = bf16[32,32,512]{2,1,0:T(8,128)(2,1)S(1)} custom-call(bf16[32,144,128]{2,1,0:T(8,128)(2,1)S(1)} %all-to-all-done.2.back, bf16[32,128,128]{2,1,0:T(8,128)(2,1)S(1)} %get-tuple-element.17.numer_ref, f32[32,8,128]{2,1,0:T(8,128)S(1)} %get-tuple-element.18.stat_ref), custom_call_target="tpu_custom_call" | custom-call | tf_op jit(solution)/shard_map/merge/pallas_call | solution.py:369
  151.2 1.1 reshape.97
  (26 shorter events, 0.1 us)
Async XLA Ops:
  0.0 1.3 copy-start.4
  1.3 4.6 %copy-start.8 = (s32[1,32]{1,0:T(1,128)S(1)}, s32[1,32]{1,0:T(1,128)}, u32[]{:S(2)}) copy-start(s32[1,32]{1,0:T(1,128)} %param.14) | copy-start | bytes 388
  1.3 4.6 %copy-start.9 = (s32[1,32]{1,0:T(1,128)S(1)}, s32[1,32]{1,0:T(1,128)}, u32[]{:S(2)}) copy-start(s32[1,32]{1,0:T(1,128)} %param.15) | copy-start | bytes 388
  1.3 4.7 %copy-start.10 = (s32[1,8]{1,0:T(1,128)S(1)}, s32[1,8]{1,0:T(1,128)}, u32[]{:S(2)}) copy-start(s32[1,8]{1,0:T(1,128)} %param.13) | copy-start | bytes 100
  2.5 26.2 %collective-permute-start.2 = (bf16[128,5120]{1,0:T(8,128)(2,1)S(1)}, bf16[128,5120]{1,0:T(8,128)(2,1)}, u32[]{:S(2)}, u32[]{:S(2)}) collective-permute-start(bf16[128,5120]{1,0:T(8,128)(2,1)S(1)} %norm.1.refs_0_), channel_id=1, source_target_pairs={{0,1},{1,0},{2,3},{3,2},{4,5},{5,4},{6,7},{7,6},{8,9},{9,8},{10,11... | collective-permute-start | bytes 3932168 | tf_op jit(solution)/shard_map/ppermute | solution.py:298
  2.6 34.3 %collective-permute-start.1 = (bf16[128,5120]{1,0:T(8,128)(2,1)S(1)}, bf16[128,5120]{1,0:T(8,128)(2,1)}, u32[]{:S(2)}, u32[]{:S(2)}) collective-permute-start(bf16[128,5120]{1,0:T(8,128)(2,1)S(1)} %norm.1.refs_0_), channel_id=1, source_target_pairs={{0,6},{1,7},{2,0},{3,1},{4,2},{5,3},{6,4},{7,5},{8,14},{9,15},{10,... | collective-permute-start | bytes 3932168 | tf_op jit(solution)/shard_map/ppermute | solution.py:297
  3.5 33.4 %collective-permute-start = (bf16[128,5120]{1,0:T(8,128)(2,1)S(1)}, bf16[128,5120]{1,0:T(8,128)(2,1)}, u32[]{:S(2)}, u32[]{:S(2)}) collective-permute-start(bf16[128,5120]{1,0:T(8,128)(2,1)S(1)} %norm.1.refs_0_), channel_id=1, source_target_pairs={{0,2},{1,3},{2,4},{3,5},{4,6},{5,7},{6,0},{7,1},{8,10},{9,11},{10,... | collective-permute-start | bytes 3932168 | tf_op jit(solution)/shard_map/ppermute | solution.py:296
  6.8 21.2 %all-to-all-start = ((s32[32,1,1]{2,1,0:T(1,128)}), s32[32,1,1]{2,1,0:T(1,128)S(1)}, u32[]{:S(2)}, u32[]{:S(2)}) async-start(s32[32,1,1]{2,1,0:T(1,128)} %copy.12), calls=%async_computation | async-start | bytes 32768 | tf_op jit(solution)/shard_map/all_to_all | solution.py:278
  18.7 25.3 %slice-start = ((s8[5242880]{0:T(1024)(128)(4,1)}), s8[1048576]{0:T(1024)(128)(4,1)S(1)}, s32[]{:S(2)}) async-start(s8[5242880]{0:T(1024)(128)(4,1)} %bitcast.11), calls=%async_computation.3 | async-start | bytes 2097152
  28.7 2.5 %copy-start = (bf16[5120,512]{1,0:T(8,128)(2,1)S(1)}, bf16[5120,512]{1,0:T(8,128)(2,1)}, u32[]{:S(2)}) copy-start(bf16[5120,512]{1,0:T(8,128)(2,1)} %refs_2_.5) | copy-start | bytes 15728644
  31.1 1.7 %copy-start.1 = (bf16[640,8,2,128]{3,1,2,0:T(8,128)(2,1)S(1)}, bf16[640,8,2,128]{3,1,2,0:T(8,128)(2,1)}, u32[]{:S(2)}) copy-start(bf16[640,8,2,128]{3,1,2,0:T(8,128)(2,1)} %copy.15) | copy-start | bytes 7864324
  32.9 11.1 %slice-start.1 = ((s8[5242880]{0:T(1024)(128)(4,1)}), s8[4194304]{0:T(1024)(128)(4,1)S(1)}, s32[]{:S(2)}) async-start(s8[5242880]{0:T(1024)(128)(4,1)} %bitcast.11), calls=%async_computation.4 | async-start | bytes 8388608
  36.9 7.2 %copy-start.2 = (bf16[640,8,2,128]{3,1,2,0:T(8,128)(2,1)S(1)}, bf16[640,8,2,128]{3,1,2,0:T(8,128)(2,1)}, u32[]{:S(2)}) copy-start(bf16[640,8,2,128]{3,1,2,0:T(8,128)(2,1)} %copy.15) | copy-start | bytes 7864324
  39.0 5.0 %collective-permute-start.5 = (bf16[256,5120]{1,0:T(8,128)(2,1)S(1)}, bf16[256,5120]{1,0:T(8,128)(2,1)S(1)}, u32[]{:S(2)}, u32[]{:S(2)}) collective-permute-start(bf16[256,5120]{1,0:T(8,128)(2,1)S(1)} %get-tuple-element.14.refs_0_), channel_id=1, source_target_pairs={{0,1},{1,0},{2,3},{3,2},{4,5},{5,4},{6,7},{7,6},{8,9},{9,8},{10,11... | collective-permute-start | bytes 7864328 | tf_op jit(solution)/shard_map/ppermute | solution.py:324
  39.1 17.1 %collective-permute-start.3 = (bf16[64,5120]{1,0:T(8,128)(2,1)S(1)}, bf16[64,5120]{1,0:T(8,128)(2,1)S(1)}, u32[]{:S(2)}, u32[]{:S(2)}) collective-permute-start(bf16[64,5120]{1,0:T(8,128)(2,1)S(1)} %get-tuple-element.12), channel_id=1, source_target_pairs={{0,2},{1,3},{2,4},{3,5},{4,6},{5,7},{6,0},{7,1},{8,10},{9,11},{10,... | collective-permute-start | bytes 1966088 | tf_op jit(solution)/shard_map/ppermute | solution.py:322
  40.2 18.0 %collective-permute-start.4 = (bf16[64,5120]{1,0:T(8,128)(2,1)S(1)}, bf16[64,5120]{1,0:T(8,128)(2,1)S(1)}, u32[]{:S(2)}, u32[]{:S(2)}) collective-permute-start(bf16[64,5120]{1,0:T(8,128)(2,1)S(1)} %get-tuple-element.13), channel_id=1, source_target_pairs={{0,6},{1,7},{2,0},{3,1},{4,2},{5,3},{6,4},{7,5},{8,14},{9,15},{10,... | collective-permute-start | bytes 1966088 | tf_op jit(solution)/shard_map/ppermute | solution.py:323
  58.3 3.1 %collective-permute-start.6 = (bf16[128,5120]{1,0:T(8,128)(2,1)S(1)}, bf16[128,5120]{1,0:T(8,128)(2,1)S(1)}, u32[]{:S(2)}, u32[]{:S(2)}) collective-permute-start(bf16[128,5120]{1,0:T(8,128)(2,1)S(1)} %join.1.refs_0_), channel_id=1, source_target_pairs={{0,1},{1,0},{2,3},{3,2},{4,5},{5,4},{6,7},{7,6},{8,9},{9,8},{10,11... | collective-permute-start | bytes 3932168 | tf_op jit(solution)/shard_map/ppermute | solution.py:335
  65.5 0.8 copy-start.5
  66.3 11.7 %copy-start.7 = (s32[1,32]{1,0:T(1,128)S(1)}, s32[1,32]{1,0:T(1,128)}, u32[]{:S(2)}) copy-start(s32[1,32]{1,0:T(1,128)} %param.12) | copy-start | bytes 388
  66.3 40.5 %copy-start.3 = (bf16[32,2,128,128]{3,2,1,0:T(8,128)(2,1)S(1)}, bf16[32,2,128,128]{3,2,1,0:T(8,128)(2,1)}, u32[]{:S(2)}) copy-start(bf16[32,2,128,128]{3,2,1,0:T(8,128)(2,1)} %pages.1) | copy-start | bytes 6291460
  66.3 40.5 %all-to-all-start.1 = ((bf16[32,128,128]{2,1,0:T(8,128)(2,1)}), bf16[32,128,128]{2,1,0:T(8,128)(2,1)S(1)}, u32[]{:S(2)}, u32[]{:S(2)}) async-start(bf16[32,128,128]{2,1,0:T(8,128)(2,1)} %get-tuple-element.15.queries), calls=%async_computation.1 | async-start | bytes 2097152 | tf_op jit(solution)/shard_map/all_to_all | solution.py:348
  113.1 5.2 %copy-start.6 = (bf16[32,64,128]{2,1,0:T(8,128)(2,1)S(1)}, bf16[32,64,128]{2,1,0:T(8,128)(2,1)}, u32[]{:S(2)}) copy-start(bf16[32,64,128]{2,1,0:T(8,128)(2,1)} %copy-done.5) | copy-start | bytes 1572868
  113.1 36.2 %all-to-all-start.2 = ((bf16[32,144,128]{2,1,0:T(8,128)(2,1)}), bf16[32,144,128]{2,1,0:T(8,128)(2,1)S(1)}, u32[]{:S(2)}, u32[]{:S(2)}) async-start(bf16[32,144,128]{2,1,0:T(8,128)(2,1)} %prompt_attention.1), calls=%async_computation.2 | async-start | bytes 2359296 | tf_op jit(solution)/shard_map/all_to_all | solution.py:368
where the time goes:
time: 153 us; the launch traced here: 152 us
  waiting for transfers between devices  76.4 us (50%)
  starting transfers between devices  34 us (22%)
  Pallas kernels  28.2 us (18%)
  local copies, waits for them, and re-layouts  12.1 us (8%)
    all_to_all x1, waiting for transfers between devices, body(): lax.all_to_all(queries, 'dp', split_axis=0, concat_axis=0, tiled=True)  28.4 us
    all_to_all x1, waiting for transfers between devices, body(): lax.all_to_all(answers, 'dp', split_axis=0, concat_axis=0, tiled=True)  27.8 us
    all_to_all x1, starting transfers between devices, body(): lax.all_to_all(queries, 'dp', split_axis=0, concat_axis=0, tiled=True)  11.6 us
    all_to_all x1, starting transfers between devices, body(): lax.all_to_all(dest_count, 'dp', split_axis=0, concat_axis=0, tiled=True)  11.5 us
    unnamed x27, local copies, waits for them, and re-layouts  10 us
    pallas_call x2, Pallas kernels, project_near(): pl.pallas_call(functools.partial(near_kernel, deltas), out_shape=jax.Shap...  9.39 us
    ppermute x1, waiting for transfers between devices, body(): far_0 = lax.ppermute(far_0, 'tensor', along_x(1))  6.8 us
    pallas_call x1, Pallas kernels, body(): pl.pallas_call(prompt_kernel, out_shape=jax.ShapeDtypeStruct((OWNERS, TIL...  6.24 us
  transfers between devices with their start and end apart: 10, of which 7 were waited for; matrix products, arithmetic and copies ran while one was open for 4% of the time, Pallas kernels for 8%

commit v1 on v0

--- a/solution.py
+++ b/solution.py
@@ -20,7 +20,7 @@
 OWNERS = 32
 HEADS = 4
 TILE = HEADS * SLAB
-STAT_ROWS = 16
+STAT_ROWS = 8
 MiB = 1024 * 1024
 
 
@@ -173,7 +173,7 @@
     scale = math.log2(math.e) / math.sqrt(HEAD_SIZE)
 
     def some(step, carry):
-        groups = [step * 4 + i for i in range(4)]
+        groups = [step * 16 + i for i in range(16)]
         at = [[tables[g * LONGEST_PAGES + page] for page in range(LONGEST_PAGES)] for g in groups]
         scores = []
         for i, g in enumerate(groups):
@@ -193,17 +193,17 @@
         for i, g in enumerate(groups):
             values = jnp.concatenate([pages[p, 1] for p in at[i]], axis=0)
             numer = jnp.dot(mass[i].astype(jnp.bfloat16), values, preferred_element_type=jnp.float32)
-            answers[g, pl.ds(0, TILE), :] = (numer / total[i]).astype(jnp.bfloat16)
+            numer = numer / total[i]
             flat = jnp.sum(jnp.where(eye, logs[i], 0.0), axis=0, keepdims=True)
             stats = jnp.zeros((STAT_ROWS, HEAD_SIZE), jnp.float32)
             for piece in range(3):
                 rounded = flat.astype(jnp.bfloat16).astype(jnp.float32)
                 stats = jnp.where(row == piece, rounded, stats)
                 flat = flat - rounded
-            answers[g, pl.ds(TILE, STAT_ROWS), :] = stats.astype(jnp.bfloat16)
+            answers[g] = jnp.concatenate([numer, stats], axis=0).astype(jnp.bfloat16)
         return carry
 
-    lax.fori_loop(0, OWNERS // 4, some, 0)
+    lax.fori_loop(0, OWNERS // 16, some, 0)
 
 
 def merge_kernel(back, numer_ref, stat_ref, out):
@@ -212,7 +212,8 @@
     def some(step, carry):
         for i in range(4):
             owner = step * 4 + i
-            stats = back[owner, pl.ds(TILE, STAT_ROWS), :].astype(jnp.float32)
+            message = back[owner].astype(jnp.float32)
+            stats = message[TILE:]
             log_p = stats[0:1] + (stats[1:2] + stats[2:3])
             peak_n, total_n = stat_ref[owner, 0:1, :], stat_ref[owner, 1:2, :]
             log_n = peak_n + jnp.log(total_n)
@@ -222,11 +223,13 @@
             share_n = second / ((first + second) * total_n)
             share_p = jnp.sum(jnp.where(eye, share_p, 0.0), axis=1, keepdims=True)
             share_n = jnp.sum(jnp.where(eye, share_n, 0.0), axis=1, keepdims=True)
-            prompt = back[owner, pl.ds(0, TILE), :].astype(jnp.float32)
+            prompt = message[:TILE]
             newest = numer_ref[owner].astype(jnp.float32)
-            merged = (prompt * share_p + newest * share_n).astype(jnp.bfloat16)
+            merged = (prompt * share_p + newest * share_n)
             for j in range(HEADS):
-                out[owner, :, pl.ds(j * HEAD_SIZE, HEAD_SIZE)] = merged[j * SLAB:(j + 1) * SLAB]
+                rows = merged[j * SLAB:(j + 1) * SLAB].reshape(PROMPT_SAMPLES, STEPS, HEAD_SIZE)
+                samples = pl.ds(owner * PROMPT_SAMPLES, PROMPT_SAMPLES)
+                out[samples, :, pl.ds(j * HEAD_SIZE, HEAD_SIZE)] = rows.astype(jnp.bfloat16)
         return carry
 
     lax.fori_loop(0, OWNERS // 4, some, 0)
@@ -366,15 +369,16 @@
         name="prompt_attention",
     )(physical, dest_count, asked, keyvalue_pages)
     back = lax.all_to_all(answers, "dp", split_axis=0, concat_axis=0, tiled=True)
-    out = pl.pallas_call(
+    return pl.pallas_call(
         merge_kernel,
-        out_shape=jax.ShapeDtypeStruct((OWNERS, SLAB, HEADS * HEAD_SIZE), jnp.bfloat16),
+        out_shape=jax.ShapeDtypeStruct(
+            (groups * PROMPT_SAMPLES, STEPS, HEADS * HEAD_SIZE), jnp.bfloat16
+        ),
         in_specs=[VMEM] * 3,
         out_specs=VMEM,
         compiler_params=params(8),
         name="merge",
     )(back, *newest)
-    return out.reshape(groups * PROMPT_SAMPLES, STEPS, HEADS * HEAD_SIZE)
 
 
 def solution(mesh):

time: 153 us -> 150 us (0.980)
  no operation moved by 1% of the time
where the time goes in v1:
time: 150 us
  waiting for transfers between devices  75 us (50%)
  starting transfers between devices  34 us (23%)
  Pallas kernels  28.3 us (19%)
  local copies, waits for them, and re-layouts  10.9 us (7%)
    all_to_all x1, waiting for transfers between devices, body(): lax.all_to_all(queries, 'dp', split_axis=0, concat_axis=0, tiled=True)  28.4 us
    all_to_all x1, waiting for transfers between devices, body(): lax.all_to_all(answers, 'dp', split_axis=0, concat_axis=0, tiled=True)  26.4 us
    all_to_all x1, starting transfers between devices, body(): lax.all_to_all(queries, 'dp', split_axis=0, concat_axis=0, tiled=True)  11.6 us
    all_to_all x1, starting transfers between devices, body(): lax.all_to_all(dest_count, 'dp', split_axis=0, concat_axis=0, tiled=True)  11.5 us
    unnamed x27, local copies, waits for them, and re-layouts  10 us
    pallas_call x2, Pallas kernels, project_near(): pl.pallas_call(functools.partial(near_kernel, deltas), out_shape=jax.Shap...  9.39 us
    ppermute x1, waiting for transfers between devices, body(): far_0 = lax.ppermute(far_0, 'tensor', along_x(1))  6.8 us
    all_to_all x1, waiting for transfers between devices, body(): lax.all_to_all(dest_count, 'dp', split_axis=0, concat_axis=0, tiled=True)  5.61 us
  transfers between devices with their start and end apart: 10, of which 7 were waited for; matrix products, arithmetic and copies ran while one was open for 4% of the time, Pallas kernels for 8%

profile of v1, /device:TPU:6, one launch (start us, length us, event | category | flops | bytes accessed | tf_op | source)
XLA Modules:
  0.0 150.0 jit_solution(7376891007677130396)
XLA Ops:
  0.0 1.3 copy-done.4
  1.3 1.1 norm.1.refs_0_
  2.5 0.1 collective-permute-start.2
  2.6 0.9 collective-permute-start.1
  3.5 2.4 %collective-permute-start = (bf16[128,5120]{1,0:T(8,128)(2,1)S(1)}, bf16[128,5120]{1,0:T(8,128)(2,1)}, u32[]{:S(2)}, u32[]{:S(2)}) collective-permute-start(bf16[128,5120]{1,0:T(8,128)(2,1)S(1)} %norm.1.refs_0_), channel_id=1, source_target_pairs={{0,2},{1,3},{2,4},{3,5},{4,6},{5,7},{6,0},{7,1},{8,10},{9,11},{10,... | collective-permute-start | bytes 3932168 | tf_op jit(solution)/shard_map/ppermute | solution.py:299
  5.9 0.1 select_reduce_fusion.1
  6.0 0.1 select_reduce_fusion.2.counts
  6.1 0.7 copy.12
  6.8 11.5 %all-to-all-start = ((s32[32,1,1]{2,1,0:T(1,128)}), s32[32,1,1]{2,1,0:T(1,128)S(1)}, u32[]{:S(2)}, u32[]{:S(2)}) async-start(s32[32,1,1]{2,1,0:T(1,128)} %copy.12), calls=%async_computation | async-start | bytes 32768 | tf_op jit(solution)/shard_map/all_to_all | solution.py:281
  18.3 0.1 add_convert_fusion
  18.4 0.1 fusion
  18.5 0.1 pad_maximum_fusion
  18.6 0.1 pad_add_fusion.place
  18.7 3.7 %copy.15 = bf16[640,8,2,128]{3,1,2,0:T(8,128)(2,1)} copy(bf16[640,8,2,128]{3,2,1,0:T(2,128)(2,1)} %bitcast.17) | data formatting | bytes 5242880
  22.4 5.6 %all-to-all-done = s32[32,1,1]{2,1,0:T(1,128)S(1)} async-done(((s32[32,1,1]{2,1,0:T(1,128)}), s32[32,1,1]{2,1,0:T(1,128)S(1)}, u32[]{:S(2)}, u32[]{:S(2)}) %all-to-all-start) | async-done | bytes 160 | tf_op jit(solution)/shard_map/all_to_all | solution.py:281
  28.0 0.7 reduce.counts
  28.6 0.0 collective-permute-done.2.refs_1_
  28.7 0.0 copy-start
  28.7 2.5 %copy-done = bf16[5120,512]{1,0:T(8,128)(2,1)S(1)} copy-done((bf16[5120,512]{1,0:T(8,128)(2,1)S(1)}, bf16[5120,512]{1,0:T(8,128)(2,1)}, u32[]{:S(2)}) %copy-start) | copy-done | bytes 5242904
  31.1 1.7 %copy-done.1 = bf16[640,8,2,128]{3,1,2,0:T(8,128)(2,1)S(1)} copy-done((bf16[640,8,2,128]{3,1,2,0:T(8,128)(2,1)S(1)}, bf16[640,8,2,128]{3,1,2,0:T(8,128)(2,1)}, u32[]{:S(2)}) %copy-start.1) | copy-done | bytes 2621464
  32.9 4.0 %project_near.2.refs_0_.refs_6_ = bf16[1,8,192,128]{3,2,1,0:T(8,128)(2,1)S(1)} custom-call(s32[2]{0:T(128)S(1)} %pad_add_fusion.place, s32[32]{0:T(128)S(1)} %reduce.counts, bf16[128,5120]{1,0:T(8,128)(2,1)S(1)} %norm.1.refs_0_, bf16[128,5120]{1,0:T(8,128)(2,1)} %collective-permute-done.2.refs_1_, bf16[5120,512]{1,0:T(8,128)(2,1)S(1)} %copy-done, ...), custom_call_target="tpu_custom_call" | custom-call | tf_op jit(solution)/shard_map/project_near/pallas_call | solution.py:304
  36.9 0.0 copy-start.2
  36.9 0.0 collective-permute-done.1.behind
  36.9 0.0 collective-permute-done.ahead
  36.9 2.1 %forward.1 = (bf16[256,5120]{1,0:T(8,128)(2,1)S(1)}, bf16[64,5120]{1,0:T(8,128)(2,1)S(1)}, bf16[64,5120]{1,0:T(8,128)(2,1)S(1)}) custom-call(bf16[128,5120]{1,0:T(8,128)(2,1)} %collective-permute-done.ahead, bf16[128,5120]{1,0:T(8,128)(2,1)} %collective-permute-done.1.behind, bf16[1,8,192,128]{3,2,1,0:T(8,128)(2,1)S(1)} %project_near.2.refs_0_.refs_6_), custom_call_target="tpu_custom_call" | custom-call | tf_op jit(solution)/shard_map/forward/pallas_call | solution.py:317
  39.0 0.1 collective-permute-start.5
  39.1 1.1 collective-permute-start.3
  40.2 1.0 collective-permute-start.4
  41.2 2.8 %collective-permute-done.5.refs_1_ = bf16[256,5120]{1,0:T(8,128)(2,1)S(1)} collective-permute-done((bf16[256,5120]{1,0:T(8,128)(2,1)S(1)}, bf16[256,5120]{1,0:T(8,128)(2,1)S(1)}, u32[]{:S(2)}, u32[]{:S(2)}) %collective-permute-start.5) | collective-permute-done | bytes 2621472 | tf_op jit(solution)/shard_map/ppermute | solution.py:327
  44.0 5.4 %project_near.3.after.refs_7_ = bf16[2,8,192,128]{3,2,1,0:T(8,128)(2,1)S(1)} custom-call(s32[2]{0:T(128)S(1)} %pad_add_fusion.place, s32[32]{0:T(128)S(1)} %reduce.counts, bf16[256,5120]{1,0:T(8,128)(2,1)S(1)} %get-tuple-element.14.refs_0_, bf16[256,5120]{1,0:T(8,128)(2,1)S(1)} %collective-permute-done.5.refs_1_, bf16[5120,512]{1,0:T(8,128)(2,1)S(1)} %bitcast.12, ...), custom_call_target="tpu_custom_call" | custom-call | tf_op jit(solution)/shard_map/project_near/pallas_call | solution.py:304
  49.5 6.8 %collective-permute-done.3.far_0 = bf16[64,5120]{1,0:T(8,128)(2,1)S(1)} collective-permute-done((bf16[64,5120]{1,0:T(8,128)(2,1)S(1)}, bf16[64,5120]{1,0:T(8,128)(2,1)S(1)}, u32[]{:S(2)}, u32[]{:S(2)}) %collective-permute-start.3) | collective-permute-done | bytes 655392 | tf_op jit(solution)/shard_map/ppermute | solution.py:325
  56.3 1.9 %collective-permute-done.4.far_1 = bf16[64,5120]{1,0:T(8,128)(2,1)S(1)} collective-permute-done((bf16[64,5120]{1,0:T(8,128)(2,1)S(1)}, bf16[64,5120]{1,0:T(8,128)(2,1)S(1)}, u32[]{:S(2)}, u32[]{:S(2)}) %collective-permute-start.4) | collective-permute-done | bytes 655392 | tf_op jit(solution)/shard_map/ppermute | solution.py:326
  58.2 0.1 join.1.refs_0_
  58.3 0.1 collective-permute-start.6
  58.4 3.0 %collective-permute-done.6.refs_1_ = bf16[128,5120]{1,0:T(8,128)(2,1)S(1)} collective-permute-done((bf16[128,5120]{1,0:T(8,128)(2,1)S(1)}, bf16[128,5120]{1,0:T(8,128)(2,1)S(1)}, u32[]{:S(2)}, u32[]{:S(2)}) %collective-permute-start.6) | collective-permute-done | bytes 1310752 | tf_op jit(solution)/shard_map/ppermute | solution.py:338
  61.4 4.1 %project_far.1 = (bf16[32,128,128]{2,1,0:T(8,128)(2,1)}, bf16[32,64,128]{2,1,0:T(8,128)(2,1)S(1)}) custom-call(s32[2]{0:T(128)S(1)} %pad_add_fusion.place, s32[32]{0:T(128)S(1)} %reduce.counts, bf16[128,5120]{1,0:T(8,128)(2,1)S(1)} %join.1.refs_0_, bf16[128,5120]{1,0:T(8,128)(2,1)S(1)} %collective-permute-done.6.refs_1_, bf16[5120,512]{1,0:T(8,128)(2,1)S(1)} %bitcast.12, ...), custom_call_target="tpu_custom_call" | custom-call | tf_op jit(solution)/shard_map/project_far/pallas_call | solution.py:339
  65.5 0.8 copy-done.5
  66.3 11.6 %all-to-all-start.1 = ((bf16[32,128,128]{2,1,0:T(8,128)(2,1)}), bf16[32,128,128]{2,1,0:T(8,128)(2,1)S(1)}, u32[]{:S(2)}, u32[]{:S(2)}) async-start(bf16[32,128,128]{2,1,0:T(8,128)(2,1)} %get-tuple-element.15.queries), calls=%async_computation.1 | async-start | bytes 2097152 | tf_op jit(solution)/shard_map/all_to_all | solution.py:351
  77.9 0.2 select_reduce_fusion
  78.2 0.1 copy.11
  78.3 0.1 reshape.92.tables
  78.4 28.4 %all-to-all-done.1.queries = bf16[32,128,128]{2,1,0:T(8,128)(2,1)S(1)} async-done(((bf16[32,128,128]{2,1,0:T(8,128)(2,1)}), bf16[32,128,128]{2,1,0:T(8,128)(2,1)S(1)}, u32[]{:S(2)}, u32[]{:S(2)}) %all-to-all-start.1) | async-done | bytes 1048608 | tf_op jit(solution)/shard_map/all_to_all | solution.py:351
  106.8 0.0 copy-done.3
  106.8 5.4 %prompt_attention.1 = bf16[32,136,128]{2,1,0:T(8,128)(2,1)} custom-call(s32[128]{0:T(128)S(1)} %reshape.92.tables, s32[32]{0:T(128)S(1)} %select_reduce_fusion.2.counts, bf16[32,128,128]{2,1,0:T(8,128)(2,1)S(1)} %all-to-all-done.1.queries, bf16[32,2,128,128]{3,2,1,0:T(8,128)(2,1)S(1)} %copy-done.3), custom_call_target="tpu_custom_call" | custom-call | tf_op jit(solution)/shard_map/prompt_attention/pallas_call | solution.py:363
  112.2 5.2 %all-to-all-start.2 = ((bf16[32,136,128]{2,1,0:T(8,128)(2,1)}), bf16[32,136,128]{2,1,0:T(8,128)(2,1)S(1)}, u32[]{:S(2)}, u32[]{:S(2)}) async-start(bf16[32,136,128]{2,1,0:T(8,128)(2,1)} %prompt_attention.1), calls=%async_computation.2 | async-start | bytes 2228224 | tf_op jit(solution)/shard_map/all_to_all | solution.py:371
  117.5 3.2 %newest_tokens.1 = (bf16[32,128,128]{2,1,0:T(8,128)(2,1)S(1)}, f32[32,8,128]{2,1,0:T(8,128)S(1)}) custom-call(bf16[32,128,128]{2,1,0:T(8,128)(2,1)} %get-tuple-element.15.queries, bf16[32,64,128]{2,1,0:T(8,128)(2,1)S(1)} %copy-done.6), custom_call_target="tpu_custom_call" | custom-call | tf_op jit(solution)/shard_map/newest_tokens/pallas_call | solution.py:352
  120.7 26.4 %all-to-all-done.2.back = bf16[32,136,128]{2,1,0:T(8,128)(2,1)S(1)} async-done(((bf16[32,136,128]{2,1,0:T(8,128)(2,1)}), bf16[32,136,128]{2,1,0:T(8,128)(2,1)S(1)}, u32[]{:S(2)}, u32[]{:S(2)}) %all-to-all-start.2) | async-done | bytes 1114144 | tf_op jit(solution)/shard_map/all_to_all | solution.py:371
  147.1 2.9 %merge.1 = bf16[256,4,512]{2,1,0:T(4,128)(2,1)} custom-call(bf16[32,136,128]{2,1,0:T(8,128)(2,1)S(1)} %all-to-all-done.2.back, bf16[32,128,128]{2,1,0:T(8,128)(2,1)S(1)} %get-tuple-element.17.numer_ref, f32[32,8,128]{2,1,0:T(8,128)S(1)} %get-tuple-element.18.stat_ref), custom_call_target="tpu_custom_call" | custom-call | tf_op jit(solution)/shard_map/merge/pallas_call | solution.py:372
  (25 shorter events, 0.1 us)
Async XLA Ops:
  0.0 1.3 copy-start.4
  1.3 4.6 %copy-start.8 = (s32[1,32]{1,0:T(1,128)S(1)}, s32[1,32]{1,0:T(1,128)}, u32[]{:S(2)}) copy-start(s32[1,32]{1,0:T(1,128)} %param.14) | copy-start | bytes 388
  1.3 4.6 %copy-start.9 = (s32[1,32]{1,0:T(1,128)S(1)}, s32[1,32]{1,0:T(1,128)}, u32[]{:S(2)}) copy-start(s32[1,32]{1,0:T(1,128)} %param.15) | copy-start | bytes 388
  1.3 4.7 %copy-start.10 = (s32[1,8]{1,0:T(1,128)S(1)}, s32[1,8]{1,0:T(1,128)}, u32[]{:S(2)}) copy-start(s32[1,8]{1,0:T(1,128)} %param.13) | copy-start | bytes 100
  2.5 26.2 %collective-permute-start.2 = (bf16[128,5120]{1,0:T(8,128)(2,1)S(1)}, bf16[128,5120]{1,0:T(8,128)(2,1)}, u32[]{:S(2)}, u32[]{:S(2)}) collective-permute-start(bf16[128,5120]{1,0:T(8,128)(2,1)S(1)} %norm.1.refs_0_), channel_id=1, source_target_pairs={{0,1},{1,0},{2,3},{3,2},{4,5},{5,4},{6,7},{7,6},{8,9},{9,8},{10,11... | collective-permute-start | bytes 3932168 | tf_op jit(solution)/shard_map/ppermute | solution.py:301
  2.6 34.3 %collective-permute-start.1 = (bf16[128,5120]{1,0:T(8,128)(2,1)S(1)}, bf16[128,5120]{1,0:T(8,128)(2,1)}, u32[]{:S(2)}, u32[]{:S(2)}) collective-permute-start(bf16[128,5120]{1,0:T(8,128)(2,1)S(1)} %norm.1.refs_0_), channel_id=1, source_target_pairs={{0,6},{1,7},{2,0},{3,1},{4,2},{5,3},{6,4},{7,5},{8,14},{9,15},{10,... | collective-permute-start | bytes 3932168 | tf_op jit(solution)/shard_map/ppermute | solution.py:300
  3.5 33.4 %collective-permute-start = (bf16[128,5120]{1,0:T(8,128)(2,1)S(1)}, bf16[128,5120]{1,0:T(8,128)(2,1)}, u32[]{:S(2)}, u32[]{:S(2)}) collective-permute-start(bf16[128,5120]{1,0:T(8,128)(2,1)S(1)} %norm.1.refs_0_), channel_id=1, source_target_pairs={{0,2},{1,3},{2,4},{3,5},{4,6},{5,7},{6,0},{7,1},{8,10},{9,11},{10,... | collective-permute-start | bytes 3932168 | tf_op jit(solution)/shard_map/ppermute | solution.py:299
  6.8 21.2 %all-to-all-start = ((s32[32,1,1]{2,1,0:T(1,128)}), s32[32,1,1]{2,1,0:T(1,128)S(1)}, u32[]{:S(2)}, u32[]{:S(2)}) async-start(s32[32,1,1]{2,1,0:T(1,128)} %copy.12), calls=%async_computation | async-start | bytes 32768 | tf_op jit(solution)/shard_map/all_to_all | solution.py:281
  18.7 25.3 %slice-start = ((s8[5242880]{0:T(1024)(128)(4,1)}), s8[1048576]{0:T(1024)(128)(4,1)S(1)}, s32[]{:S(2)}) async-start(s8[5242880]{0:T(1024)(128)(4,1)} %bitcast.11), calls=%async_computation.3 | async-start | bytes 2097152
  28.7 2.5 %copy-start = (bf16[5120,512]{1,0:T(8,128)(2,1)S(1)}, bf16[5120,512]{1,0:T(8,128)(2,1)}, u32[]{:S(2)}) copy-start(bf16[5120,512]{1,0:T(8,128)(2,1)} %refs_2_.5) | copy-start | bytes 15728644
  31.1 1.7 %copy-start.1 = (bf16[640,8,2,128]{3,1,2,0:T(8,128)(2,1)S(1)}, bf16[640,8,2,128]{3,1,2,0:T(8,128)(2,1)}, u32[]{:S(2)}) copy-start(bf16[640,8,2,128]{3,1,2,0:T(8,128)(2,1)} %copy.15) | copy-start | bytes 7864324
  32.9 11.1 %slice-start.1 = ((s8[5242880]{0:T(1024)(128)(4,1)}), s8[4194304]{0:T(1024)(128)(4,1)S(1)}, s32[]{:S(2)}) async-start(s8[5242880]{0:T(1024)(128)(4,1)} %bitcast.11), calls=%async_computation.4 | async-start | bytes 8388608
  36.9 7.2 %copy-start.2 = (bf16[640,8,2,128]{3,1,2,0:T(8,128)(2,1)S(1)}, bf16[640,8,2,128]{3,1,2,0:T(8,128)(2,1)}, u32[]{:S(2)}) copy-start(bf16[640,8,2,128]{3,1,2,0:T(8,128)(2,1)} %copy.15) | copy-start | bytes 7864324
  39.0 5.0 %collective-permute-start.5 = (bf16[256,5120]{1,0:T(8,128)(2,1)S(1)}, bf16[256,5120]{1,0:T(8,128)(2,1)S(1)}, u32[]{:S(2)}, u32[]{:S(2)}) collective-permute-start(bf16[256,5120]{1,0:T(8,128)(2,1)S(1)} %get-tuple-element.14.refs_0_), channel_id=1, source_target_pairs={{0,1},{1,0},{2,3},{3,2},{4,5},{5,4},{6,7},{7,6},{8,9},{9,8},{10,11... | collective-permute-start | bytes 7864328 | tf_op jit(solution)/shard_map/ppermute | solution.py:327
  39.1 17.1 %collective-permute-start.3 = (bf16[64,5120]{1,0:T(8,128)(2,1)S(1)}, bf16[64,5120]{1,0:T(8,128)(2,1)S(1)}, u32[]{:S(2)}, u32[]{:S(2)}) collective-permute-start(bf16[64,5120]{1,0:T(8,128)(2,1)S(1)} %get-tuple-element.12), channel_id=1, source_target_pairs={{0,2},{1,3},{2,4},{3,5},{4,6},{5,7},{6,0},{7,1},{8,10},{9,11},{10,... | collective-permute-start | bytes 1966088 | tf_op jit(solution)/shard_map/ppermute | solution.py:325
  40.2 18.0 %collective-permute-start.4 = (bf16[64,5120]{1,0:T(8,128)(2,1)S(1)}, bf16[64,5120]{1,0:T(8,128)(2,1)S(1)}, u32[]{:S(2)}, u32[]{:S(2)}) collective-permute-start(bf16[64,5120]{1,0:T(8,128)(2,1)S(1)} %get-tuple-element.13), channel_id=1, source_target_pairs={{0,6},{1,7},{2,0},{3,1},{4,2},{5,3},{6,4},{7,5},{8,14},{9,15},{10,... | collective-permute-start | bytes 1966088 | tf_op jit(solution)/shard_map/ppermute | solution.py:326
  58.3 3.1 %collective-permute-start.6 = (bf16[128,5120]{1,0:T(8,128)(2,1)S(1)}, bf16[128,5120]{1,0:T(8,128)(2,1)S(1)}, u32[]{:S(2)}, u32[]{:S(2)}) collective-permute-start(bf16[128,5120]{1,0:T(8,128)(2,1)S(1)} %join.1.refs_0_), channel_id=1, source_target_pairs={{0,1},{1,0},{2,3},{3,2},{4,5},{5,4},{6,7},{7,6},{8,9},{9,8},{10,11... | collective-permute-start | bytes 3932168 | tf_op jit(solution)/shard_map/ppermute | solution.py:338
  65.5 0.8 copy-start.5
  66.3 11.7 %copy-start.7 = (s32[1,32]{1,0:T(1,128)S(1)}, s32[1,32]{1,0:T(1,128)}, u32[]{:S(2)}) copy-start(s32[1,32]{1,0:T(1,128)} %param.12) | copy-start | bytes 388
  66.3 40.5 %copy-start.3 = (bf16[32,2,128,128]{3,2,1,0:T(8,128)(2,1)S(1)}, bf16[32,2,128,128]{3,2,1,0:T(8,128)(2,1)}, u32[]{:S(2)}) copy-start(bf16[32,2,128,128]{3,2,1,0:T(8,128)(2,1)} %pages.1) | copy-start | bytes 6291460
  66.3 40.5 %all-to-all-start.1 = ((bf16[32,128,128]{2,1,0:T(8,128)(2,1)}), bf16[32,128,128]{2,1,0:T(8,128)(2,1)S(1)}, u32[]{:S(2)}, u32[]{:S(2)}) async-start(bf16[32,128,128]{2,1,0:T(8,128)(2,1)} %get-tuple-element.15.queries), calls=%async_computation.1 | async-start | bytes 2097152 | tf_op jit(solution)/shard_map/all_to_all | solution.py:351
  112.2 5.3 %copy-start.6 = (bf16[32,64,128]{2,1,0:T(8,128)(2,1)S(1)}, bf16[32,64,128]{2,1,0:T(8,128)(2,1)}, u32[]{:S(2)}) copy-start(bf16[32,64,128]{2,1,0:T(8,128)(2,1)} %copy-done.5) | copy-start | bytes 1572868
  112.2 34.8 %all-to-all-start.2 = ((bf16[32,136,128]{2,1,0:T(8,128)(2,1)}), bf16[32,136,128]{2,1,0:T(8,128)(2,1)S(1)}, u32[]{:S(2)}, u32[]{:S(2)}) async-start(bf16[32,136,128]{2,1,0:T(8,128)(2,1)} %prompt_attention.1), calls=%async_computation.2 | async-start | bytes 2228224 | tf_op jit(solution)/shard_map/all_to_all | solution.py:371

commit v2 on v1

--- a/solution.py
+++ b/solution.py
@@ -166,7 +166,7 @@
     lax.fori_loop(0, OWNERS // 8, some, 0)
 
 
-def prompt_kernel(tables, counts, queries, pages, answers):
+def prompt_kernel(tables, counts, queries, pages, after, answers):
     eye = diagonal()
     row = lax.broadcasted_iota(jnp.int32, (STAT_ROWS, HEAD_SIZE), 0)
     token = lax.broadcasted_iota(jnp.int32, (TILE, LONGEST_PAGES * PAGE_TOKENS), 1)
@@ -210,8 +210,8 @@
     eye = diagonal()
 
     def some(step, carry):
-        for i in range(4):
-            owner = step * 4 + i
+        for i in range(16):
+            owner = step * 16 + i
             message = back[owner].astype(jnp.float32)
             stats = message[TILE:]
             log_p = stats[0:1] + (stats[1:2] + stats[2:3])
@@ -232,7 +232,7 @@
                 out[samples, :, pl.ds(j * HEAD_SIZE, HEAD_SIZE)] = rows.astype(jnp.bfloat16)
         return carry
 
-    lax.fori_loop(0, OWNERS // 4, some, 0)
+    lax.fori_loop(0, OWNERS // 16, some, 0)
 
 
 def diagonal():
@@ -363,11 +363,11 @@
     answers = pl.pallas_call(
         prompt_kernel,
         out_shape=jax.ShapeDtypeStruct((OWNERS, TILE + STAT_ROWS, HEAD_SIZE), jnp.bfloat16),
-        in_specs=[SMEM] * 2 + [VMEM] * 2,
+        in_specs=[SMEM] * 2 + [VMEM] * 3,
         out_specs=VMEM,
         compiler_params=params(8),
         name="prompt_attention",
-    )(physical, dest_count, asked, keyvalue_pages)
+    )(physical, dest_count, asked, keyvalue_pages, newest[1])
     back = lax.all_to_all(answers, "dp", split_axis=0, concat_axis=0, tiled=True)
     return pl.pallas_call(
         merge_kernel,

time: 150 us -> 150 us (level)
  blocking collectives: 0 us -> 36.2 us
  waiting for transfers between devices: 75 us -> 43.3 us
  starting transfers between devices: 34 us -> 28.8 us
  local copies, waits for them, and re-layouts: 10.9 us -> 13 us
  Pallas kernels: 28.3 us -> 26.7 us
    all_to_all x0 -> x1, blocking collectives: none -> 36.2 us  [body(): lax.all_to_all(answers, 'dp', split_axis=0, concat_axis=0, tiled=True)]
    all_to_all x1 -> x0, waiting for transfers between devices: 26.4 us -> none  [body(): lax.all_to_all(answers, 'dp', split_axis=0, concat_axis=0, tiled=True)]
    all_to_all x1, waiting for transfers between devices: 28.4 us -> 23.2 us  [body(): lax.all_to_all(queries, 'dp', split_axis=0, concat_axis=0, tiled=True)]
    all_to_all x1 -> x0, starting transfers between devices: 5.24 us -> none  [body(): lax.all_to_all(answers, 'dp', split_axis=0, concat_axis=0, tiled=True)]
    unnamed x27 -> x31, local copies, waits for them, and re-layouts: 10 us -> 12.1 us
  transfers between devices with their start and end apart: 10 -> 9, of which waited for: 7 -> 6; matrix products, arithmetic and copies ran while one was open for 4% -> 4% of each run, Pallas kernels for 8% -> 8%
where the time goes in v2:
time: 150 us
  waiting for transfers between devices  43.3 us (29%)
  blocking collectives  36.2 us (24%)
  starting transfers between devices  28.8 us (19%)
  Pallas kernels  26.7 us (18%)
  local copies, waits for them, and re-layouts  13 us (9%)
    all_to_all x1, blocking collectives, body(): lax.all_to_all(answers, 'dp', split_axis=0, concat_axis=0, tiled=True)  36.2 us
    all_to_all x1, waiting for transfers between devices, body(): lax.all_to_all(queries, 'dp', split_axis=0, concat_axis=0, tiled=True)  23.2 us
    unnamed x31, local copies, waits for them, and re-layouts  12.1 us
    all_to_all x1, starting transfers between devices, body(): lax.all_to_all(queries, 'dp', split_axis=0, concat_axis=0, tiled=True)  11.6 us
    all_to_all x1, starting transfers between devices, body(): lax.all_to_all(dest_count, 'dp', split_axis=0, concat_axis=0, tiled=True)  11.5 us
    pallas_call x2, Pallas kernels, project_near(): pl.pallas_call(functools.partial(near_kernel, deltas), out_shape=jax.Shap...  9.39 us
    ppermute x1, waiting for transfers between devices, body(): far_0 = lax.ppermute(far_0, 'tensor', along_x(1))  6.8 us
    all_to_all x1, waiting for transfers between devices, body(): lax.all_to_all(dest_count, 'dp', split_axis=0, concat_axis=0, tiled=True)  5.61 us
  transfers between devices with their start and end apart: 9, of which 6 were waited for; matrix products, arithmetic and copies ran while one was open for 4% of the time, Pallas kernels for 8%

profile of v2, /device:TPU:6, one launch (start us, length us, event | category | flops | bytes accessed | tf_op | source)
XLA Modules:
  0.0 149.7 jit_solution(4074528521803689030)
XLA Ops:
  0.0 1.3 copy-done.4
  1.3 1.1 norm.1.refs_0_
  2.5 0.1 collective-permute-start.2
  2.6 0.9 collective-permute-start.1
  3.5 2.4 %collective-permute-start = (bf16[128,5120]{1,0:T(8,128)(2,1)S(1)}, bf16[128,5120]{1,0:T(8,128)(2,1)}, u32[]{:S(2)}, u32[]{:S(2)}) collective-permute-start(bf16[128,5120]{1,0:T(8,128)(2,1)S(1)} %norm.1.refs_0_), channel_id=1, source_target_pairs={{0,2},{1,3},{2,4},{3,5},{4,6},{5,7},{6,0},{7,1},{8,10},{9,11},{10,... | collective-permute-start | bytes 3932168 | tf_op jit(solution)/shard_map/ppermute | solution.py:299
  5.9 0.0 copy-done.11
  5.9 0.1 select_reduce_fusion.1
  6.0 0.1 select_reduce_fusion.2.counts
  6.1 0.7 copy.12
  6.8 11.5 %all-to-all-start = ((s32[32,1,1]{2,1,0:T(1,128)}), s32[32,1,1]{2,1,0:T(1,128)S(1)}, u32[]{:S(2)}, u32[]{:S(2)}) async-start(s32[32,1,1]{2,1,0:T(1,128)} %copy.12), calls=%async_computation | async-start | bytes 32768 | tf_op jit(solution)/shard_map/all_to_all | solution.py:281
  18.3 0.1 add_convert_fusion
  18.4 0.1 fusion
  18.5 0.1 pad_maximum_fusion
  18.6 0.1 pad_add_fusion.place
  18.7 3.7 %copy.15 = bf16[640,8,2,128]{3,1,2,0:T(8,128)(2,1)} copy(bf16[640,8,2,128]{3,2,1,0:T(2,128)(2,1)} %bitcast.17) | data formatting | bytes 5242880
  22.4 5.6 %all-to-all-done = s32[32,1,1]{2,1,0:T(1,128)S(1)} async-done(((s32[32,1,1]{2,1,0:T(1,128)}), s32[32,1,1]{2,1,0:T(1,128)S(1)}, u32[]{:S(2)}, u32[]{:S(2)}) %all-to-all-start) | async-done | bytes 160 | tf_op jit(solution)/shard_map/all_to_all | solution.py:281
  28.0 0.7 reduce.counts
  28.6 0.0 collective-permute-done.2.refs_1_
  28.7 0.0 copy-start
  28.7 2.5 %copy-done = bf16[5120,512]{1,0:T(8,128)(2,1)S(1)} copy-done((bf16[5120,512]{1,0:T(8,128)(2,1)S(1)}, bf16[5120,512]{1,0:T(8,128)(2,1)}, u32[]{:S(2)}) %copy-start) | copy-done | bytes 5242904
  31.1 1.7 %copy-done.1 = bf16[640,8,2,128]{3,1,2,0:T(8,128)(2,1)S(1)} copy-done((bf16[640,8,2,128]{3,1,2,0:T(8,128)(2,1)S(1)}, bf16[640,8,2,128]{3,1,2,0:T(8,128)(2,1)}, u32[]{:S(2)}) %copy-start.1) | copy-done | bytes 2621464
  32.9 4.0 %project_near.2.refs_0_.refs_6_ = bf16[1,8,192,128]{3,2,1,0:T(8,128)(2,1)S(1)} custom-call(s32[2]{0:T(128)S(1)} %pad_add_fusion.place, s32[32]{0:T(128)S(1)} %reduce.counts, bf16[128,5120]{1,0:T(8,128)(2,1)S(1)} %norm.1.refs_0_, bf16[128,5120]{1,0:T(8,128)(2,1)} %collective-permute-done.2.refs_1_, bf16[5120,512]{1,0:T(8,128)(2,1)S(1)} %copy-done, ...), custom_call_target="tpu_custom_call" | custom-call | tf_op jit(solution)/shard_map/project_near/pallas_call | solution.py:304
  36.9 0.0 collective-permute-done.1.behind
  36.9 0.0 collective-permute-done.ahead
  36.9 2.1 %forward.1 = (bf16[256,5120]{1,0:T(8,128)(2,1)S(1)}, bf16[64,5120]{1,0:T(8,128)(2,1)S(1)}, bf16[64,5120]{1,0:T(8,128)(2,1)S(1)}) custom-call(bf16[128,5120]{1,0:T(8,128)(2,1)} %collective-permute-done.ahead, bf16[128,5120]{1,0:T(8,128)(2,1)} %collective-permute-done.1.behind, bf16[1,8,192,128]{3,2,1,0:T(8,128)(2,1)S(1)} %project_near.2.refs_0_.refs_6_), custom_call_target="tpu_custom_call" | custom-call | tf_op jit(solution)/shard_map/forward/pallas_call | solution.py:317
  39.0 0.1 collective-permute-start.5
  39.1 1.1 collective-permute-start.3
  40.2 1.0 collective-permute-start.4
  41.2 2.8 %collective-permute-done.5.refs_1_ = bf16[256,5120]{1,0:T(8,128)(2,1)S(1)} collective-permute-done((bf16[256,5120]{1,0:T(8,128)(2,1)S(1)}, bf16[256,5120]{1,0:T(8,128)(2,1)S(1)}, u32[]{:S(2)}, u32[]{:S(2)}) %collective-permute-start.5) | collective-permute-done | bytes 2621472 | tf_op jit(solution)/shard_map/ppermute | solution.py:327
  44.0 5.4 %project_near.3.after.refs_7_ = bf16[2,8,192,128]{3,2,1,0:T(8,128)(2,1)S(1)} custom-call(s32[2]{0:T(128)S(1)} %pad_add_fusion.place, s32[32]{0:T(128)S(1)} %reduce.counts, bf16[256,5120]{1,0:T(8,128)(2,1)S(1)} %get-tuple-element.14.refs_0_, bf16[256,5120]{1,0:T(8,128)(2,1)S(1)} %collective-permute-done.5.refs_1_, bf16[5120,512]{1,0:T(8,128)(2,1)S(1)} %bitcast.12, ...), custom_call_target="tpu_custom_call" | custom-call | tf_op jit(solution)/shard_map/project_near/pallas_call | solution.py:304
  49.5 6.8 %collective-permute-done.3.far_0 = bf16[64,5120]{1,0:T(8,128)(2,1)S(1)} collective-permute-done((bf16[64,5120]{1,0:T(8,128)(2,1)S(1)}, bf16[64,5120]{1,0:T(8,128)(2,1)S(1)}, u32[]{:S(2)}, u32[]{:S(2)}) %collective-permute-start.3) | collective-permute-done | bytes 655392 | tf_op jit(solution)/shard_map/ppermute | solution.py:325
  56.3 1.9 %collective-permute-done.4.far_1 = bf16[64,5120]{1,0:T(8,128)(2,1)S(1)} collective-permute-done((bf16[64,5120]{1,0:T(8,128)(2,1)S(1)}, bf16[64,5120]{1,0:T(8,128)(2,1)S(1)}, u32[]{:S(2)}, u32[]{:S(2)}) %collective-permute-start.4) | collective-permute-done | bytes 655392 | tf_op jit(solution)/shard_map/ppermute | solution.py:326
  58.2 0.1 join.1.refs_0_
  58.3 0.1 collective-permute-start.6
  58.4 3.0 %collective-permute-done.6.refs_1_ = bf16[128,5120]{1,0:T(8,128)(2,1)S(1)} collective-permute-done((bf16[128,5120]{1,0:T(8,128)(2,1)S(1)}, bf16[128,5120]{1,0:T(8,128)(2,1)S(1)}, u32[]{:S(2)}, u32[]{:S(2)}) %collective-permute-start.6) | collective-permute-done | bytes 1310752 | tf_op jit(solution)/shard_map/ppermute | solution.py:338
  61.4 4.1 %project_far.1 = (bf16[32,128,128]{2,1,0:T(8,128)(2,1)}, bf16[32,64,128]{2,1,0:T(8,128)(2,1)S(1)}) custom-call(s32[2]{0:T(128)S(1)} %pad_add_fusion.place, s32[32]{0:T(128)S(1)} %reduce.counts, bf16[128,5120]{1,0:T(8,128)(2,1)S(1)} %join.1.refs_0_, bf16[128,5120]{1,0:T(8,128)(2,1)S(1)} %collective-permute-done.6.refs_1_, bf16[5120,512]{1,0:T(8,128)(2,1)S(1)} %bitcast.12, ...), custom_call_target="tpu_custom_call" | custom-call | tf_op jit(solution)/shard_map/project_far/pallas_call | solution.py:339
  65.5 0.8 copy-done.7
  66.3 11.6 %all-to-all-start.1 = ((bf16[32,128,128]{2,1,0:T(8,128)(2,1)}), bf16[32,128,128]{2,1,0:T(8,128)(2,1)S(1)}, u32[]{:S(2)}, u32[]{:S(2)}) async-start(bf16[32,128,128]{2,1,0:T(8,128)(2,1)} %get-tuple-element.15.queries), calls=%async_computation.1 | async-start | bytes 2097152 | tf_op jit(solution)/shard_map/all_to_all | solution.py:351
  77.9 0.2 select_reduce_fusion
  78.2 0.1 copy.11
  78.3 0.1 reshape.92.tables
  78.4 1.0 copy-done.8
  79.4 3.2 %newest_tokens.1 = (bf16[32,128,128]{2,1,0:T(8,128)(2,1)S(1)}, f32[32,8,128]{2,1,0:T(8,128)S(1)}) custom-call(bf16[32,128,128]{2,1,0:T(8,128)(2,1)} %get-tuple-element.15.queries, bf16[32,64,128]{2,1,0:T(8,128)(2,1)S(1)} %copy-done.8), custom_call_target="tpu_custom_call" | custom-call | tf_op jit(solution)/shard_map/newest_tokens/pallas_call | solution.py:352
  82.6 1.0 copy-done.5
  83.6 23.2 %all-to-all-done.1.queries = bf16[32,128,128]{2,1,0:T(8,128)(2,1)S(1)} async-done(((bf16[32,128,128]{2,1,0:T(8,128)(2,1)}), bf16[32,128,128]{2,1,0:T(8,128)(2,1)S(1)}, u32[]{:S(2)}, u32[]{:S(2)}) %all-to-all-start.1) | async-done | bytes 1048608 | tf_op jit(solution)/shard_map/all_to_all | solution.py:351
  106.8 4.4 %prompt_attention.1 = bf16[32,136,128]{2,1,0:T(8,128)(2,1)S(1)} custom-call(s32[128]{0:T(128)S(1)} %reshape.92.tables, s32[32]{0:T(128)S(1)} %select_reduce_fusion.2.counts, bf16[32,128,128]{2,1,0:T(8,128)(2,1)S(1)} %all-to-all-done.1.queries, bf16[32,2,128,128]{3,2,1,0:T(8,128)(2,1)S(1)} %copy-done.3, f32[32,8,128]{2,1,0:T(8,128)S(1)} %get-tuple-element.17.after.stat_ref), custom_call_target="tpu_custom_call" | custom-call | tf_op jit(solution)/shard_map/prompt_attention/pallas_call | solution.py:363
  111.2 36.2 %all_to_all.21.back = bf16[32,136,128]{2,1,0:T(8,128)(2,1)S(1)} all-to-all(bf16[32,136,128]{2,1,0:T(8,128)(2,1)S(1)} %prompt_attention.1), channel_id=1, replica_groups=mesh['dp'=32,'tensor'=8] {'dp'}, dimensions={0} | all-to-all | bytes 2228224 | tf_op jit(solution)/shard_map/all_to_all | solution.py:371
  147.4 2.3 %merge.1 = bf16[256,4,512]{2,1,0:T(4,128)(2,1)} custom-call(bf16[32,136,128]{2,1,0:T(8,128)(2,1)S(1)} %all_to_all.21.back, bf16[32,128,128]{2,1,0:T(8,128)(2,1)S(1)} %copy-done.6, f32[32,8,128]{2,1,0:T(8,128)S(1)} %get-tuple-element.17.after.stat_ref), custom_call_target="tpu_custom_call" | custom-call | tf_op jit(solution)/shard_map/merge/pallas_call | solution.py:372
  (28 shorter events, 0.1 us)
Async XLA Ops:
  0.0 1.3 copy-start.4
  1.3 4.6 %copy-start.10 = (s32[1,32]{1,0:T(1,128)S(1)}, s32[1,32]{1,0:T(1,128)}, u32[]{:S(2)}) copy-start(s32[1,32]{1,0:T(1,128)} %param.14) | copy-start | bytes 388
  1.3 4.6 %copy-start.11 = (s32[1,32]{1,0:T(1,128)S(1)}, s32[1,32]{1,0:T(1,128)}, u32[]{:S(2)}) copy-start(s32[1,32]{1,0:T(1,128)} %param.15) | copy-start | bytes 388
  1.3 4.7 %copy-start.12 = (s32[1,8]{1,0:T(1,128)S(1)}, s32[1,8]{1,0:T(1,128)}, u32[]{:S(2)}) copy-start(s32[1,8]{1,0:T(1,128)} %param.13) | copy-start | bytes 100
  2.5 26.2 %collective-permute-start.2 = (bf16[128,5120]{1,0:T(8,128)(2,1)S(1)}, bf16[128,5120]{1,0:T(8,128)(2,1)}, u32[]{:S(2)}, u32[]{:S(2)}) collective-permute-start(bf16[128,5120]{1,0:T(8,128)(2,1)S(1)} %norm.1.refs_0_), channel_id=1, source_target_pairs={{0,1},{1,0},{2,3},{3,2},{4,5},{5,4},{6,7},{7,6},{8,9},{9,8},{10,11... | collective-permute-start | bytes 3932168 | tf_op jit(solution)/shard_map/ppermute | solution.py:301
  2.6 34.3 %collective-permute-start.1 = (bf16[128,5120]{1,0:T(8,128)(2,1)S(1)}, bf16[128,5120]{1,0:T(8,128)(2,1)}, u32[]{:S(2)}, u32[]{:S(2)}) collective-permute-start(bf16[128,5120]{1,0:T(8,128)(2,1)S(1)} %norm.1.refs_0_), channel_id=1, source_target_pairs={{0,6},{1,7},{2,0},{3,1},{4,2},{5,3},{6,4},{7,5},{8,14},{9,15},{10,... | collective-permute-start | bytes 3932168 | tf_op jit(solution)/shard_map/ppermute | solution.py:300
  3.5 33.4 %collective-permute-start = (bf16[128,5120]{1,0:T(8,128)(2,1)S(1)}, bf16[128,5120]{1,0:T(8,128)(2,1)}, u32[]{:S(2)}, u32[]{:S(2)}) collective-permute-start(bf16[128,5120]{1,0:T(8,128)(2,1)S(1)} %norm.1.refs_0_), channel_id=1, source_target_pairs={{0,2},{1,3},{2,4},{3,5},{4,6},{5,7},{6,0},{7,1},{8,10},{9,11},{10,... | collective-permute-start | bytes 3932168 | tf_op jit(solution)/shard_map/ppermute | solution.py:299
  6.8 21.2 %all-to-all-start = ((s32[32,1,1]{2,1,0:T(1,128)}), s32[32,1,1]{2,1,0:T(1,128)S(1)}, u32[]{:S(2)}, u32[]{:S(2)}) async-start(s32[32,1,1]{2,1,0:T(1,128)} %copy.12), calls=%async_computation | async-start | bytes 32768 | tf_op jit(solution)/shard_map/all_to_all | solution.py:281
  18.7 25.3 %slice-start = ((s8[5242880]{0:T(1024)(128)(4,1)}), s8[1048576]{0:T(1024)(128)(4,1)S(1)}, s32[]{:S(2)}) async-start(s8[5242880]{0:T(1024)(128)(4,1)} %bitcast.11), calls=%async_computation.3 | async-start | bytes 2097152
  28.7 2.5 %copy-start = (bf16[5120,512]{1,0:T(8,128)(2,1)S(1)}, bf16[5120,512]{1,0:T(8,128)(2,1)}, u32[]{:S(2)}) copy-start(bf16[5120,512]{1,0:T(8,128)(2,1)} %refs_2_.5) | copy-start | bytes 15728644
  31.1 1.7 %copy-start.1 = (bf16[640,8,2,128]{3,1,2,0:T(8,128)(2,1)S(1)}, bf16[640,8,2,128]{3,1,2,0:T(8,128)(2,1)}, u32[]{:S(2)}) copy-start(bf16[640,8,2,128]{3,1,2,0:T(8,128)(2,1)} %copy.15) | copy-start | bytes 7864324
  32.9 11.1 %slice-start.1 = ((s8[5242880]{0:T(1024)(128)(4,1)}), s8[4194304]{0:T(1024)(128)(4,1)S(1)}, s32[]{:S(2)}) async-start(s8[5242880]{0:T(1024)(128)(4,1)} %bitcast.11), calls=%async_computation.4 | async-start | bytes 8388608
  36.9 7.2 %copy-start.2 = (bf16[640,8,2,128]{3,1,2,0:T(8,128)(2,1)S(1)}, bf16[640,8,2,128]{3,1,2,0:T(8,128)(2,1)}, u32[]{:S(2)}) copy-start(bf16[640,8,2,128]{3,1,2,0:T(8,128)(2,1)} %copy.15) | copy-start | bytes 7864324
  39.0 5.0 %collective-permute-start.5 = (bf16[256,5120]{1,0:T(8,128)(2,1)S(1)}, bf16[256,5120]{1,0:T(8,128)(2,1)S(1)}, u32[]{:S(2)}, u32[]{:S(2)}) collective-permute-start(bf16[256,5120]{1,0:T(8,128)(2,1)S(1)} %get-tuple-element.14.refs_0_), channel_id=1, source_target_pairs={{0,1},{1,0},{2,3},{3,2},{4,5},{5,4},{6,7},{7,6},{8,9},{9,8},{10,11... | collective-permute-start | bytes 7864328 | tf_op jit(solution)/shard_map/ppermute | solution.py:327
  39.1 17.1 %collective-permute-start.3 = (bf16[64,5120]{1,0:T(8,128)(2,1)S(1)}, bf16[64,5120]{1,0:T(8,128)(2,1)S(1)}, u32[]{:S(2)}, u32[]{:S(2)}) collective-permute-start(bf16[64,5120]{1,0:T(8,128)(2,1)S(1)} %get-tuple-element.12), channel_id=1, source_target_pairs={{0,2},{1,3},{2,4},{3,5},{4,6},{5,7},{6,0},{7,1},{8,10},{9,11},{10,... | collective-permute-start | bytes 1966088 | tf_op jit(solution)/shard_map/ppermute | solution.py:325
  40.2 18.0 %collective-permute-start.4 = (bf16[64,5120]{1,0:T(8,128)(2,1)S(1)}, bf16[64,5120]{1,0:T(8,128)(2,1)S(1)}, u32[]{:S(2)}, u32[]{:S(2)}) collective-permute-start(bf16[64,5120]{1,0:T(8,128)(2,1)S(1)} %get-tuple-element.13), channel_id=1, source_target_pairs={{0,6},{1,7},{2,0},{3,1},{4,2},{5,3},{6,4},{7,5},{8,14},{9,15},{10,... | collective-permute-start | bytes 1966088 | tf_op jit(solution)/shard_map/ppermute | solution.py:326
  58.3 3.1 %collective-permute-start.6 = (bf16[128,5120]{1,0:T(8,128)(2,1)S(1)}, bf16[128,5120]{1,0:T(8,128)(2,1)S(1)}, u32[]{:S(2)}, u32[]{:S(2)}) collective-permute-start(bf16[128,5120]{1,0:T(8,128)(2,1)S(1)} %join.1.refs_0_), channel_id=1, source_target_pairs={{0,1},{1,0},{2,3},{3,2},{4,5},{5,4},{6,7},{7,6},{8,9},{9,8},{10,11... | collective-permute-start | bytes 3932168 | tf_op jit(solution)/shard_map/ppermute | solution.py:338
  65.5 0.8 copy-start.7
  66.3 11.7 %copy-start.9 = (s32[1,32]{1,0:T(1,128)S(1)}, s32[1,32]{1,0:T(1,128)}, u32[]{:S(2)}) copy-start(s32[1,32]{1,0:T(1,128)} %param.12) | copy-start | bytes 388
  66.3 40.5 %copy-start.3 = (bf16[32,2,128,128]{3,2,1,0:T(8,128)(2,1)S(1)}, bf16[32,2,128,128]{3,2,1,0:T(8,128)(2,1)}, u32[]{:S(2)}) copy-start(bf16[32,2,128,128]{3,2,1,0:T(8,128)(2,1)} %pages.1) | copy-start | bytes 6291460
  66.3 40.5 %all-to-all-start.1 = ((bf16[32,128,128]{2,1,0:T(8,128)(2,1)}), bf16[32,128,128]{2,1,0:T(8,128)(2,1)S(1)}, u32[]{:S(2)}, u32[]{:S(2)}) async-start(bf16[32,128,128]{2,1,0:T(8,128)(2,1)} %get-tuple-element.15.queries), calls=%async_computation.1 | async-start | bytes 2097152 | tf_op jit(solution)/shard_map/all_to_all | solution.py:351
  78.4 1.0 copy-start.8
  82.6 1.0 copy-start.5
  111.2 36.2 %copy-start.6 = (bf16[32,128,128]{2,1,0:T(8,128)(2,1)S(1)}, bf16[32,128,128]{2,1,0:T(8,128)(2,1)}, u32[]{:S(2)}) copy-start(bf16[32,128,128]{2,1,0:T(8,128)(2,1)} %copy-done.5) | copy-start | bytes 3145732

commit v3 on v2

--- a/solution.py
+++ b/solution.py
@@ -55,12 +55,9 @@
     return out.reshape(SLAB, HEAD_SIZE)
 
 
-def norm_kernel(states, slab, held, scratch, sem):
-    load = pltpu.make_async_copy(states, held, sem)
-    load.start()
-    load.wait()
+def norm_kernel(states, slab, scratch):
     for r in range(states.shape[0]):
-        flat = held[r].astype(jnp.float32)
+        flat = states[r].astype(jnp.float32)
         flat = flat * lax.rsqrt(jnp.mean(flat * flat, axis=-1, keepdims=True) + EPSILON)
         scratch[r * STEPS:(r + 1) * STEPS, :] = flat
     slab[...] = scratch[...].astype(jnp.bfloat16)
@@ -286,13 +283,9 @@
     own = pl.pallas_call(
         norm_kernel,
         out_shape=jax.ShapeDtypeStruct((rows, width), jnp.bfloat16),
-        in_specs=[ANY],
+        in_specs=[VMEM],
         out_specs=VMEM,
-        scratch_shapes=[
-            pltpu.VMEM(new_states.shape, jnp.bfloat16),
-            pltpu.VMEM((rows, width), jnp.float32),
-            pltpu.SemaphoreType.DMA,
-        ],
+        scratch_shapes=[pltpu.VMEM((rows, width), jnp.float32)],
         compiler_params=params(8),
         name="norm",
     )(new_states)

time: 150 us -> 150 us (level)
  no operation moved by 1% of the time
where the time goes in v3:
time: 150 us
  waiting for transfers between devices  43.4 us (29%)
  blocking collectives  36.2 us (24%)
  starting transfers between devices  28.8 us (19%)
  Pallas kernels  26.6 us (18%)
  local copies, waits for them, and re-layouts  13 us (9%)
    all_to_all x1, blocking collectives, body(): lax.all_to_all(answers, 'dp', split_axis=0, concat_axis=0, tiled=True)  36.2 us
    all_to_all x1, waiting for transfers between devices, body(): lax.all_to_all(queries, 'dp', split_axis=0, concat_axis=0, tiled=True)  23.2 us
    unnamed x31, local copies, waits for them, and re-layouts  12.1 us
    all_to_all x1, starting transfers between devices, body(): lax.all_to_all(queries, 'dp', split_axis=0, concat_axis=0, tiled=True)  11.6 us
    all_to_all x1, starting transfers between devices, body(): lax.all_to_all(dest_count, 'dp', split_axis=0, concat_axis=0, tiled=True)  11.5 us
    pallas_call x2, Pallas kernels, project_near(): pl.pallas_call(functools.partial(near_kernel, deltas), out_shape=jax.Shap...  9.39 us
    ppermute x1, waiting for transfers between devices, body(): far_0 = lax.ppermute(far_0, 'tensor', along_x(1))  6.8 us
    all_to_all x1, waiting for transfers between devices, body(): lax.all_to_all(dest_count, 'dp', split_axis=0, concat_axis=0, tiled=True)  5.61 us
  transfers between devices with their start and end apart: 9, of which 6 were waited for; matrix products, arithmetic and copies ran while one was open for 4% of the time, Pallas kernels for 8%

profile of v3, /device:TPU:6, one launch (start us, length us, event | category | flops | bytes accessed | tf_op | source)
XLA Modules:
  0.0 149.6 jit_solution(15538446929909230153)
XLA Ops:
  0.0 1.3 copy-done.4
  1.3 1.0 norm.1.refs_0_
  2.4 0.1 collective-permute-start.2
  2.5 0.9 collective-permute-start.1
  3.4 2.4 %collective-permute-start = (bf16[128,5120]{1,0:T(8,128)(2,1)S(1)}, bf16[128,5120]{1,0:T(8,128)(2,1)}, u32[]{:S(2)}, u32[]{:S(2)}) collective-permute-start(bf16[128,5120]{1,0:T(8,128)(2,1)S(1)} %norm.1.refs_0_), channel_id=1, source_target_pairs={{0,2},{1,3},{2,4},{3,5},{4,6},{5,7},{6,0},{7,1},{8,10},{9,11},{10,... | collective-permute-start | bytes 3932168 | tf_op jit(solution)/shard_map/ppermute | solution.py:292
  5.8 0.1 select_reduce_fusion.1
  5.9 0.1 select_reduce_fusion.2.counts
  6.0 0.7 copy.12
  6.7 11.5 %all-to-all-start = ((s32[32,1,1]{2,1,0:T(1,128)}), s32[32,1,1]{2,1,0:T(1,128)S(1)}, u32[]{:S(2)}, u32[]{:S(2)}) async-start(s32[32,1,1]{2,1,0:T(1,128)} %copy.12), calls=%async_computation | async-start | bytes 32768 | tf_op jit(solution)/shard_map/all_to_all | solution.py:278
  18.2 0.1 add_convert_fusion
  18.3 0.1 fusion
  18.4 0.1 pad_maximum_fusion
  18.5 0.1 pad_add_fusion.place
  18.6 3.7 %copy.15 = bf16[640,8,2,128]{3,1,2,0:T(8,128)(2,1)} copy(bf16[640,8,2,128]{3,2,1,0:T(2,128)(2,1)} %bitcast.17) | data formatting | bytes 5242880
  22.3 5.6 %all-to-all-done = s32[32,1,1]{2,1,0:T(1,128)S(1)} async-done(((s32[32,1,1]{2,1,0:T(1,128)}), s32[32,1,1]{2,1,0:T(1,128)S(1)}, u32[]{:S(2)}, u32[]{:S(2)}) %all-to-all-start) | async-done | bytes 160 | tf_op jit(solution)/shard_map/all_to_all | solution.py:278
  27.9 0.7 reduce.counts
  28.5 0.0 collective-permute-done.2.refs_1_
  28.5 0.0 copy-start
  28.6 2.5 %copy-done = bf16[5120,512]{1,0:T(8,128)(2,1)S(1)} copy-done((bf16[5120,512]{1,0:T(8,128)(2,1)S(1)}, bf16[5120,512]{1,0:T(8,128)(2,1)}, u32[]{:S(2)}) %copy-start) | copy-done | bytes 5242904
  31.0 1.7 %copy-done.1 = bf16[640,8,2,128]{3,1,2,0:T(8,128)(2,1)S(1)} copy-done((bf16[640,8,2,128]{3,1,2,0:T(8,128)(2,1)S(1)}, bf16[640,8,2,128]{3,1,2,0:T(8,128)(2,1)}, u32[]{:S(2)}) %copy-start.1) | copy-done | bytes 2621464
  32.8 4.0 %project_near.2.refs_0_.refs_6_ = bf16[1,8,192,128]{3,2,1,0:T(8,128)(2,1)S(1)} custom-call(s32[2]{0:T(128)S(1)} %pad_add_fusion.place, s32[32]{0:T(128)S(1)} %reduce.counts, bf16[128,5120]{1,0:T(8,128)(2,1)S(1)} %norm.1.refs_0_, bf16[128,5120]{1,0:T(8,128)(2,1)} %collective-permute-done.2.refs_1_, bf16[5120,512]{1,0:T(8,128)(2,1)S(1)} %copy-done, ...), custom_call_target="tpu_custom_call" | custom-call | tf_op jit(solution)/shard_map/project_near/pallas_call | solution.py:297
  36.8 0.0 collective-permute-done.1.behind
  36.8 0.0 collective-permute-done.ahead
  36.8 2.1 %forward.1 = (bf16[256,5120]{1,0:T(8,128)(2,1)S(1)}, bf16[64,5120]{1,0:T(8,128)(2,1)S(1)}, bf16[64,5120]{1,0:T(8,128)(2,1)S(1)}) custom-call(bf16[128,5120]{1,0:T(8,128)(2,1)} %collective-permute-done.ahead, bf16[128,5120]{1,0:T(8,128)(2,1)} %collective-permute-done.1.behind, bf16[1,8,192,128]{3,2,1,0:T(8,128)(2,1)S(1)} %project_near.2.refs_0_.refs_6_), custom_call_target="tpu_custom_call" | custom-call | tf_op jit(solution)/shard_map/forward/pallas_call | solution.py:310
  38.9 0.1 collective-permute-start.5
  39.0 1.1 collective-permute-start.3
  40.1 1.0 collective-permute-start.4
  41.1 2.8 %collective-permute-done.5.refs_1_ = bf16[256,5120]{1,0:T(8,128)(2,1)S(1)} collective-permute-done((bf16[256,5120]{1,0:T(8,128)(2,1)S(1)}, bf16[256,5120]{1,0:T(8,128)(2,1)S(1)}, u32[]{:S(2)}, u32[]{:S(2)}) %collective-permute-start.5) | collective-permute-done | bytes 2621472 | tf_op jit(solution)/shard_map/ppermute | solution.py:320
  43.9 0.0 slice-done
  43.9 5.4 %project_near.3.after.refs_7_ = bf16[2,8,192,128]{3,2,1,0:T(8,128)(2,1)S(1)} custom-call(s32[2]{0:T(128)S(1)} %pad_add_fusion.place, s32[32]{0:T(128)S(1)} %reduce.counts, bf16[256,5120]{1,0:T(8,128)(2,1)S(1)} %get-tuple-element.14.refs_0_, bf16[256,5120]{1,0:T(8,128)(2,1)S(1)} %collective-permute-done.5.refs_1_, bf16[5120,512]{1,0:T(8,128)(2,1)S(1)} %bitcast.12, ...), custom_call_target="tpu_custom_call" | custom-call | tf_op jit(solution)/shard_map/project_near/pallas_call | solution.py:297
  49.4 6.8 %collective-permute-done.3.far_0 = bf16[64,5120]{1,0:T(8,128)(2,1)S(1)} collective-permute-done((bf16[64,5120]{1,0:T(8,128)(2,1)S(1)}, bf16[64,5120]{1,0:T(8,128)(2,1)S(1)}, u32[]{:S(2)}, u32[]{:S(2)}) %collective-permute-start.3) | collective-permute-done | bytes 655392 | tf_op jit(solution)/shard_map/ppermute | solution.py:318
  56.2 1.9 %collective-permute-done.4.far_1 = bf16[64,5120]{1,0:T(8,128)(2,1)S(1)} collective-permute-done((bf16[64,5120]{1,0:T(8,128)(2,1)S(1)}, bf16[64,5120]{1,0:T(8,128)(2,1)S(1)}, u32[]{:S(2)}, u32[]{:S(2)}) %collective-permute-start.4) | collective-permute-done | bytes 655392 | tf_op jit(solution)/shard_map/ppermute | solution.py:319
  58.1 0.1 join.1.refs_0_
  58.2 0.1 collective-permute-start.6
  58.3 3.0 %collective-permute-done.6.refs_1_ = bf16[128,5120]{1,0:T(8,128)(2,1)S(1)} collective-permute-done((bf16[128,5120]{1,0:T(8,128)(2,1)S(1)}, bf16[128,5120]{1,0:T(8,128)(2,1)S(1)}, u32[]{:S(2)}, u32[]{:S(2)}) %collective-permute-start.6) | collective-permute-done | bytes 1310752 | tf_op jit(solution)/shard_map/ppermute | solution.py:331
  61.3 4.1 %project_far.1 = (bf16[32,128,128]{2,1,0:T(8,128)(2,1)}, bf16[32,64,128]{2,1,0:T(8,128)(2,1)S(1)}) custom-call(s32[2]{0:T(128)S(1)} %pad_add_fusion.place, s32[32]{0:T(128)S(1)} %reduce.counts, bf16[128,5120]{1,0:T(8,128)(2,1)S(1)} %join.1.refs_0_, bf16[128,5120]{1,0:T(8,128)(2,1)S(1)} %collective-permute-done.6.refs_1_, bf16[5120,512]{1,0:T(8,128)(2,1)S(1)} %bitcast.12, ...), custom_call_target="tpu_custom_call" | custom-call | tf_op jit(solution)/shard_map/project_far/pallas_call | solution.py:332
  65.4 0.8 copy-done.7
  66.2 11.6 %all-to-all-start.1 = ((bf16[32,128,128]{2,1,0:T(8,128)(2,1)}), bf16[32,128,128]{2,1,0:T(8,128)(2,1)S(1)}, u32[]{:S(2)}, u32[]{:S(2)}) async-start(bf16[32,128,128]{2,1,0:T(8,128)(2,1)} %get-tuple-element.15.queries), calls=%async_computation.1 | async-start | bytes 2097152 | tf_op jit(solution)/shard_map/all_to_all | solution.py:344
  77.8 0.2 select_reduce_fusion
  78.1 0.1 copy.11
  78.2 0.1 reshape.92.tables
  78.3 1.0 copy-done.8
  79.3 3.2 %newest_tokens.1 = (bf16[32,128,128]{2,1,0:T(8,128)(2,1)S(1)}, f32[32,8,128]{2,1,0:T(8,128)S(1)}) custom-call(bf16[32,128,128]{2,1,0:T(8,128)(2,1)} %get-tuple-element.15.queries, bf16[32,64,128]{2,1,0:T(8,128)(2,1)S(1)} %copy-done.8), custom_call_target="tpu_custom_call" | custom-call | tf_op jit(solution)/shard_map/newest_tokens/pallas_call | solution.py:345
  82.5 1.0 copy-done.5
  83.5 23.2 %all-to-all-done.1.queries = bf16[32,128,128]{2,1,0:T(8,128)(2,1)S(1)} async-done(((bf16[32,128,128]{2,1,0:T(8,128)(2,1)}), bf16[32,128,128]{2,1,0:T(8,128)(2,1)S(1)}, u32[]{:S(2)}, u32[]{:S(2)}) %all-to-all-start.1) | async-done | bytes 1048608 | tf_op jit(solution)/shard_map/all_to_all | solution.py:344
  106.7 4.4 %prompt_attention.1 = bf16[32,136,128]{2,1,0:T(8,128)(2,1)S(1)} custom-call(s32[128]{0:T(128)S(1)} %reshape.92.tables, s32[32]{0:T(128)S(1)} %select_reduce_fusion.2.counts, bf16[32,128,128]{2,1,0:T(8,128)(2,1)S(1)} %all-to-all-done.1.queries, bf16[32,2,128,128]{3,2,1,0:T(8,128)(2,1)S(1)} %copy-done.3, f32[32,8,128]{2,1,0:T(8,128)S(1)} %get-tuple-element.17.after.stat_ref), custom_call_target="tpu_custom_call" | custom-call | tf_op jit(solution)/shard_map/prompt_attention/pallas_call | solution.py:356
  111.1 36.2 %all_to_all.21.back = bf16[32,136,128]{2,1,0:T(8,128)(2,1)S(1)} all-to-all(bf16[32,136,128]{2,1,0:T(8,128)(2,1)S(1)} %prompt_attention.1), channel_id=1, replica_groups=mesh['dp'=32,'tensor'=8] {'dp'}, dimensions={0} | all-to-all | bytes 2228224 | tf_op jit(solution)/shard_map/all_to_all | solution.py:364
  147.3 2.3 %merge.1 = bf16[256,4,512]{2,1,0:T(4,128)(2,1)} custom-call(bf16[32,136,128]{2,1,0:T(8,128)(2,1)S(1)} %all_to_all.21.back, bf16[32,128,128]{2,1,0:T(8,128)(2,1)S(1)} %copy-done.6, f32[32,8,128]{2,1,0:T(8,128)S(1)} %get-tuple-element.17.after.stat_ref), custom_call_target="tpu_custom_call" | custom-call | tf_op jit(solution)/shard_map/merge/pallas_call | solution.py:365
  (28 shorter events, 0.1 us)
Async XLA Ops:
  0.0 1.3 copy-start.4
  1.3 4.5 %copy-start.10 = (s32[1,32]{1,0:T(1,128)S(1)}, s32[1,32]{1,0:T(1,128)}, u32[]{:S(2)}) copy-start(s32[1,32]{1,0:T(1,128)} %param.14) | copy-start | bytes 388
  1.3 4.5 %copy-start.11 = (s32[1,32]{1,0:T(1,128)S(1)}, s32[1,32]{1,0:T(1,128)}, u32[]{:S(2)}) copy-start(s32[1,32]{1,0:T(1,128)} %param.15) | copy-start | bytes 388
  1.3 4.6 %copy-start.12 = (s32[1,8]{1,0:T(1,128)S(1)}, s32[1,8]{1,0:T(1,128)}, u32[]{:S(2)}) copy-start(s32[1,8]{1,0:T(1,128)} %param.13) | copy-start | bytes 100
  2.4 26.2 %collective-permute-start.2 = (bf16[128,5120]{1,0:T(8,128)(2,1)S(1)}, bf16[128,5120]{1,0:T(8,128)(2,1)}, u32[]{:S(2)}, u32[]{:S(2)}) collective-permute-start(bf16[128,5120]{1,0:T(8,128)(2,1)S(1)} %norm.1.refs_0_), channel_id=1, source_target_pairs={{0,1},{1,0},{2,3},{3,2},{4,5},{5,4},{6,7},{7,6},{8,9},{9,8},{10,11... | collective-permute-start | bytes 3932168 | tf_op jit(solution)/shard_map/ppermute | solution.py:294
  2.5 34.3 %collective-permute-start.1 = (bf16[128,5120]{1,0:T(8,128)(2,1)S(1)}, bf16[128,5120]{1,0:T(8,128)(2,1)}, u32[]{:S(2)}, u32[]{:S(2)}) collective-permute-start(bf16[128,5120]{1,0:T(8,128)(2,1)S(1)} %norm.1.refs_0_), channel_id=1, source_target_pairs={{0,6},{1,7},{2,0},{3,1},{4,2},{5,3},{6,4},{7,5},{8,14},{9,15},{10,... | collective-permute-start | bytes 3932168 | tf_op jit(solution)/shard_map/ppermute | solution.py:293
  3.4 33.4 %collective-permute-start = (bf16[128,5120]{1,0:T(8,128)(2,1)S(1)}, bf16[128,5120]{1,0:T(8,128)(2,1)}, u32[]{:S(2)}, u32[]{:S(2)}) collective-permute-start(bf16[128,5120]{1,0:T(8,128)(2,1)S(1)} %norm.1.refs_0_), channel_id=1, source_target_pairs={{0,2},{1,3},{2,4},{3,5},{4,6},{5,7},{6,0},{7,1},{8,10},{9,11},{10,... | collective-permute-start | bytes 3932168 | tf_op jit(solution)/shard_map/ppermute | solution.py:292
  6.7 21.2 %all-to-all-start = ((s32[32,1,1]{2,1,0:T(1,128)}), s32[32,1,1]{2,1,0:T(1,128)S(1)}, u32[]{:S(2)}, u32[]{:S(2)}) async-start(s32[32,1,1]{2,1,0:T(1,128)} %copy.12), calls=%async_computation | async-start | bytes 32768 | tf_op jit(solution)/shard_map/all_to_all | solution.py:278
  18.6 25.3 %slice-start = ((s8[5242880]{0:T(1024)(128)(4,1)}), s8[1048576]{0:T(1024)(128)(4,1)S(1)}, s32[]{:S(2)}) async-start(s8[5242880]{0:T(1024)(128)(4,1)} %bitcast.11), calls=%async_computation.3 | async-start | bytes 2097152
  28.5 2.5 %copy-start = (bf16[5120,512]{1,0:T(8,128)(2,1)S(1)}, bf16[5120,512]{1,0:T(8,128)(2,1)}, u32[]{:S(2)}) copy-start(bf16[5120,512]{1,0:T(8,128)(2,1)} %refs_2_.5) | copy-start | bytes 15728644
  31.0 1.7 %copy-start.1 = (bf16[640,8,2,128]{3,1,2,0:T(8,128)(2,1)S(1)}, bf16[640,8,2,128]{3,1,2,0:T(8,128)(2,1)}, u32[]{:S(2)}) copy-start(bf16[640,8,2,128]{3,1,2,0:T(8,128)(2,1)} %copy.15) | copy-start | bytes 7864324
  32.8 11.1 %slice-start.1 = ((s8[5242880]{0:T(1024)(128)(4,1)}), s8[4194304]{0:T(1024)(128)(4,1)S(1)}, s32[]{:S(2)}) async-start(s8[5242880]{0:T(1024)(128)(4,1)} %bitcast.11), calls=%async_computation.4 | async-start | bytes 8388608
  36.8 7.2 %copy-start.2 = (bf16[640,8,2,128]{3,1,2,0:T(8,128)(2,1)S(1)}, bf16[640,8,2,128]{3,1,2,0:T(8,128)(2,1)}, u32[]{:S(2)}) copy-start(bf16[640,8,2,128]{3,1,2,0:T(8,128)(2,1)} %copy.15) | copy-start | bytes 7864324
  38.9 5.0 %collective-permute-start.5 = (bf16[256,5120]{1,0:T(8,128)(2,1)S(1)}, bf16[256,5120]{1,0:T(8,128)(2,1)S(1)}, u32[]{:S(2)}, u32[]{:S(2)}) collective-permute-start(bf16[256,5120]{1,0:T(8,128)(2,1)S(1)} %get-tuple-element.14.refs_0_), channel_id=1, source_target_pairs={{0,1},{1,0},{2,3},{3,2},{4,5},{5,4},{6,7},{7,6},{8,9},{9,8},{10,11... | collective-permute-start | bytes 7864328 | tf_op jit(solution)/shard_map/ppermute | solution.py:320
  39.0 17.1 %collective-permute-start.3 = (bf16[64,5120]{1,0:T(8,128)(2,1)S(1)}, bf16[64,5120]{1,0:T(8,128)(2,1)S(1)}, u32[]{:S(2)}, u32[]{:S(2)}) collective-permute-start(bf16[64,5120]{1,0:T(8,128)(2,1)S(1)} %get-tuple-element.12), channel_id=1, source_target_pairs={{0,2},{1,3},{2,4},{3,5},{4,6},{5,7},{6,0},{7,1},{8,10},{9,11},{10,... | collective-permute-start | bytes 1966088 | tf_op jit(solution)/shard_map/ppermute | solution.py:318
  40.1 18.0 %collective-permute-start.4 = (bf16[64,5120]{1,0:T(8,128)(2,1)S(1)}, bf16[64,5120]{1,0:T(8,128)(2,1)S(1)}, u32[]{:S(2)}, u32[]{:S(2)}) collective-permute-start(bf16[64,5120]{1,0:T(8,128)(2,1)S(1)} %get-tuple-element.13), channel_id=1, source_target_pairs={{0,6},{1,7},{2,0},{3,1},{4,2},{5,3},{6,4},{7,5},{8,14},{9,15},{10,... | collective-permute-start | bytes 1966088 | tf_op jit(solution)/shard_map/ppermute | solution.py:319
  58.2 3.1 %collective-permute-start.6 = (bf16[128,5120]{1,0:T(8,128)(2,1)S(1)}, bf16[128,5120]{1,0:T(8,128)(2,1)S(1)}, u32[]{:S(2)}, u32[]{:S(2)}) collective-permute-start(bf16[128,5120]{1,0:T(8,128)(2,1)S(1)} %join.1.refs_0_), channel_id=1, source_target_pairs={{0,1},{1,0},{2,3},{3,2},{4,5},{5,4},{6,7},{7,6},{8,9},{9,8},{10,11... | collective-permute-start | bytes 3932168 | tf_op jit(solution)/shard_map/ppermute | solution.py:331
  65.4 0.8 copy-start.7
  66.2 11.7 %copy-start.9 = (s32[1,32]{1,0:T(1,128)S(1)}, s32[1,32]{1,0:T(1,128)}, u32[]{:S(2)}) copy-start(s32[1,32]{1,0:T(1,128)} %param.12) | copy-start | bytes 388
  66.2 40.5 %copy-start.3 = (bf16[32,2,128,128]{3,2,1,0:T(8,128)(2,1)S(1)}, bf16[32,2,128,128]{3,2,1,0:T(8,128)(2,1)}, u32[]{:S(2)}) copy-start(bf16[32,2,128,128]{3,2,1,0:T(8,128)(2,1)} %pages.1) | copy-start | bytes 6291460
  66.2 40.5 %all-to-all-start.1 = ((bf16[32,128,128]{2,1,0:T(8,128)(2,1)}), bf16[32,128,128]{2,1,0:T(8,128)(2,1)S(1)}, u32[]{:S(2)}, u32[]{:S(2)}) async-start(bf16[32,128,128]{2,1,0:T(8,128)(2,1)} %get-tuple-element.15.queries), calls=%async_computation.1 | async-start | bytes 2097152 | tf_op jit(solution)/shard_map/all_to_all | solution.py:344
  78.3 1.0 copy-start.8
  82.5 1.0 copy-start.5
  111.1 36.2 %copy-start.6 = (bf16[32,128,128]{2,1,0:T(8,128)(2,1)S(1)}, bf16[32,128,128]{2,1,0:T(8,128)(2,1)}, u32[]{:S(2)}) copy-start(bf16[32,128,128]{2,1,0:T(8,128)(2,1)} %copy-done.5) | copy-start | bytes 3145732
